TPU v7x, 128 devices: a whole 4x4x4 slice. The times are simulated.
128 devices in a mesh: gx: 32 (over z, y, core), gy: 2 (over x_hi), gz: 2 (over x_lo).
Axes of the slice: x: 4 (x_hi: 2, x_lo: 2; x = x_hi * 2 + x_lo), y: 4, z: 4, core: 2. Of those that a mesh axis runs over, the one named last changes fastest.
Arguments:
- position: float32 [3, 512, 8, 8, 256], P(None, 'gx', 'gy', 'gz'), may hold values from 0 to 1
- velocity: float32 [3, 512, 8, 8, 256], P(None, 'gx', 'gy', 'gz'), may hold values from -6 to 6
- particle_mass: float32 [512, 8, 8, 256], P('gx', 'gy', 'gz'), may hold values from 0.001953125 to 0.0078125
- smoothing: float32 [512, 8, 8, 256], P('gx', 'gy', 'gz'), may hold values from 0.2 to 0.5
- entropy: float32 [512, 8, 8, 256], P('gx', 'gy', 'gz'), may hold values from 0.5 to 2
- stored_density: float32 [512, 8, 8, 256], P('gx', 'gy', 'gz'), may hold values from 0.3 to 2
- particle_count: int32 [512, 8, 8], P('gx', 'gy', 'gz'), may hold values from 64 to 256, as said below
- active_count: int32 [512, 8, 8], P('gx', 'gy', 'gz'), may hold values from 0 to 8, as said below
- pair_side: int32 [26, 512, 8, 8], P(None, 'gx', 'gy', 'gz'), may hold values from 0 to 2, as said below
Outputs:
- density: float32 [512, 8, 8, 256], P('gx', 'gy', 'gz')
- acceleration: float32 [3, 512, 8, 8, 256], P(None, 'gx', 'gy', 'gz')
Inputs may be any that keep to these rules, and one draw needn't show every extreme that they name: `particle_count`: present particles fill the first slots of a cell. `active_count`: active particles fill the first slots of a cell; some cell has 8 of them. `pair_side`: 0: the pair does not interact; 1: this cell's side evaluates it; 2: the neighbour's side does. Entry k of cell a and entry 25 - k of the cell a + offset k agree: 0 with 0, 1 with 2, 2 with 1.
All inputs are finite; a program needn't handle non-finite values.
Results may differ from a plain program's by a relative error of at most 0.0003.
Values sent between devices are 32-bit elements; how exact they have to be, the bound alone decides.
No kernel may reach another device: no remote copies, remote signals or barrier semaphores. Data moves between devices by JAX's collectives and lax.ppermute only.
A program may use at most 320 MiB of HBM per device.

v0:
```python
import functools
import math

import jax
import jax.numpy as jnp
import numpy as np
from jax import lax
from jax.experimental import pallas as pl
from jax.experimental.pallas import tpu as pltpu
from jax.sharding import PartitionSpec as P

ACT = 8
BX, BY, BZ = 16, 4, 4
CELLS = BX * BY * BZ
EX, EY, EZ = BX + 2, BY + 2, BZ + 2
EXT = EX * EY * EZ
LANES = 768
TILES = LANES // 128
GROUPS = 2 * LANES
ROWS = 112
FLAGS = 80
LIVE = 106
SPAN = 4
BATCH_D = 4
BATCH_F = 2
NONE = CELLS
ADIABATIC = 5.0 / 3.0
HIGHEST = lax.Precision.HIGHEST
f32 = jnp.float32
i32 = jnp.int32

OFFSETS = [
    (a, b, c) for a in (-1, 0, 1) for b in (-1, 0, 1) for c in (-1, 0, 1) if (a, b, c) != (0, 0, 0)
]


def maps():
    coord = np.full((8, LANES), -9, np.int32)
    coord[:3] = -5
    source = np.full((8, LANES), -1, np.int32)
    for x in range(-1, BX + 1):
        for y in range(-1, BY + 1):
            for z in range(-1, BZ + 1):
                lane = ((x + 1) * EY + y + 1) * EZ + z + 1
                coord[0, lane], coord[1, lane], coord[2, lane] = x, y, z
                inside_y, inside_z = 0 <= y < BY, 0 <= z < BZ
                face_y = 0 if y == BY else 1
                face_z = 0 if z == BZ else 1
                def place(width_home, width_y, width_z, width_yz, starts, row):
                    if inside_y and inside_z:
                        return starts[0] + row * width_home + y * BZ + z
                    if inside_z:
                        return starts[1] + row * width_y + face_y * BZ + z
                    if inside_y:
                        return starts[2] + row * width_z + y * 2 + face_z
                    return starts[3] + row * width_yz + face_y * 2 + face_z

                if 0 <= x < BX:
                    at = place(16, 8, 8, 4, (0, 256, 384, 512), x)
                else:
                    base = 576 if x < 0 else 612
                    at = place(16, 8, 8, 4, (base, base + 16, base + 24, base + 32), 0)
                source[0, lane] = at
    return coord, source


def sent_cells():
    table = np.full((8, 384), -1, np.int32)
    for x in range(BX):
        for face in range(2):
            for z in range(BZ):
                table[0, x * 8 + face * BZ + z] = (x * BY + (0 if face == 0 else BY - 1)) * BZ + z
            for y in range(BY):
                table[0, 128 + x * 8 + y * 2 + face] = (x * BY + y) * BZ + (
                    0 if face == 0 else BZ - 1
                )
            for other in range(2):
                table[0, 256 + x * 4 + face * 2 + other] = (
                    x * BY + (0 if face == 0 else BY - 1)
                ) * BZ + (0 if other == 0 else BZ - 1)
    return table


def picked(values, source_row):
    size = values.shape[1]
    rows = lax.broadcasted_iota(i32, (size, source_row.shape[1]), 0)
    chosen = (rows == source_row).astype(f32)
    return lax.dot_general(
        values, chosen, (((1,), (0,)), ((), ())), precision=HIGHEST, preferred_element_type=f32
    )


def unit_rows():
    return (
        lax.broadcasted_iota(i32, (ACT, 128), 0) == lax.broadcasted_iota(i32, (ACT, 128), 1)
    ).astype(f32)


def cells_to_lanes(natural):
    return lax.dot_general(
        unit_rows(), natural[:, :128], (((1,), (1,)), ((), ())), precision=HIGHEST,
        preferred_element_type=f32,
    )


def lanes_to_cells(rows):
    return lax.dot_general(
        rows, unit_rows(), (((0,), (0,)), ((), ())), precision=HIGHEST, preferred_element_type=f32
    )


def live_mass(mass, count):
    slot = lax.broadcasted_iota(i32, (CELLS, 256), 1)
    return jnp.where(slot < count, mass, 0.0)


def pack_kernel(pos, vel, mass, smooth, entropy, stored, count, flags, sent, table, faces):
    fields = [pos[c].reshape(CELLS, 256) for c in range(3)]
    fields.append(live_mass(mass[...].reshape(CELLS, 256), count[...]))
    fields.append(smooth[...].reshape(CELLS, 256))
    fields += [vel[c].reshape(CELLS, 256) for c in range(3)]
    fields += [entropy[...].reshape(CELLS, 256), stored[...].reshape(CELLS, 256)]
    for f, field in enumerate(fields):
        table[8 * f : 8 * f + 8, :] = cells_to_lanes(field)
    table[FLAGS:ROWS, :] = flags[...]
    faces[...] = picked(table[...], sent[0:1, :])


def doubled(rows, group):
    swapped = pltpu.roll(rows, 4, 0)
    low = lax.broadcasted_iota(i32, rows.shape, 0) < 4
    return jnp.where(low, rows, swapped) if group == 0 else jnp.where(low, swapped, rows)


def store_rows(target, feature, rows):
    for group in range(2):
        both = doubled(rows, group)
        for t in range(TILES):
            target[feature, group * TILES + t] = both[:, 128 * t : 128 * t + 128]


def store_columns(target, feature, block, natural):
    low = lax.broadcasted_iota(i32, (8, 128), 0) < 4
    for s in range(8):
        first = jnp.broadcast_to(natural[s : s + 1, :128], (8, 128))
        second = jnp.broadcast_to(natural[s : s + 1, 128:], (8, 128))
        target[block * 8 + s, feature] = jnp.where(low, first, second)


def build_lists(table, coord, list_d, list_f, count_d, count_f):
    active = lax.broadcasted_iota(i32, (8, LANES), 0).astype(f32) < table[LIVE : LIVE + 1, :]
    reach = 4.0 * table[32:40, :] * table[32:40, :] * 1.0001
    squares = []
    for c in range(3):
        p = table[8 * c : 8 * c + 8, :]
        squares.append({-1: p * p, 0: None, 1: (1.0 - p) * (1.0 - p)})
    far = jnp.where(active, 0.0, 1e9)
    cx, cy, cz = coord[0:1, :], coord[1:2, :], coord[2:3, :]
    entries_d, entries_f = [], []
    kept_d = kept_f = jnp.zeros((2, LANES), i32)
    center = 13
    offsets = OFFSETS[:center] + [(0, 0, 0)] + OFFSETS[center:]
    for k, (ox, oy, oz) in enumerate(offsets):
        away = far
        for c, o in enumerate((ox, oy, oz)):
            if o:
                away = away + squares[c][o]
        bx, by, bz = cx + ox, cy + oy, cz + oz
        ok = (bx >= 0) & (bx < BX) & (by >= 0) & (by < BY) & (bz >= 0) & (bz < BZ)
        if k != center:
            row = FLAGS + (k if k < center else k - 1)
            ok = ok & (table[row : row + 1, :] > 0.5)
        cell = (bx * BY + by) * BZ + bz
        over_d = away - reach
        over_f = away - 1.0001

        def near(over):
            return jnp.concatenate(
                [jnp.min(over[0:4], 0, keepdims=True), jnp.min(over[4:8], 0, keepdims=True)], 0
            )

        both = jnp.concatenate([cell, cell], 0)
        oks = jnp.concatenate([ok.astype(i32), ok.astype(i32)], 0) > 0
        for over, entries, which in ((over_d, entries_d, 0), (over_f, entries_f, 1)):
            keep = oks & (near(over) <= 0.0)
            kept = kept_d if which == 0 else kept_f
            entries.append(jnp.where(keep, both + (k - kept) * 1024, NONE))
            if which == 0:
                kept_d = kept + keep.astype(i32)
            else:
                kept_f = kept + keep.astype(i32)
    for entries, target, kept, counted in (
        (entries_d, list_d, kept_d, count_d), (entries_f, list_f, kept_f, count_f),
    ):
        for bit in range(5):
            step, mask = 1 << bit, 1024 << bit
            moves = [(e & mask) != 0 for e in entries]
            moved = []
            for p in range(27):
                e = jnp.where(moves[p], NONE, entries[p])
                if p + step < 27:
                    e = jnp.where(moves[p + step], entries[p + step], e)
                moved.append(e)
            entries = moved
        entries = [e & 1023 for e in entries] + [jnp.full((2, LANES), NONE, i32)]
        for p in range(28):
            for group in range(2):
                target[p : p + 1, group * LANES : group * LANES + LANES] = entries[p][group : group + 1]
        for group in range(2):
            counted[0:1, group * LANES : group * LANES + LANES] = kept[group : group + 1]


def work_items(counts, order):
    def step(i, carry):
        at, total = carry
        for u in range(16):
            group = i * 16 + u
            items = (counts[0, group] + SPAN - 1) // SPAN
            order[at] = group + items * 65536
            at = at + (items > 0).astype(i32)
            total = total + items
        return at, total

    at, total = lax.fori_loop(0, GROUPS // 16, step, (jnp.int32(0), jnp.int32(0)))
    order[at] = (GROUPS - 1) + (1 << 30)
    return total


def run_items(total, batch, order, lists, item):
    def advance(at, done):
        entry = order[at]
        last = done + 1 >= (entry >> 16)
        return (entry & 65535) + done * 65536, jnp.where(last, at + 1, at), jnp.where(last, 0, done + 1)

    def take(at, done):
        taken = []
        for _ in range(batch):
            code, at, done = advance(at, done)
            taken.append(code)
        return at, done, taken

    at, done, first = take(jnp.int32(0), jnp.int32(0))

    def step(_, carry):
        at, done, codes = carry
        at, done, later = take(at, done)
        for code in codes:
            group, part = code & 65535, code >> 16
            cells = [lists[part * SPAN + v, group] for v in range(SPAN)]
            item(group >> 7, group & 127, cells)
        return at, done, later

    lax.fori_loop(0, (total + batch - 1) // batch, step, (at, done, first))


def lane_of(lane):
    return jnp.full((8, 128), lane, i32)


def folded(partial_first, partial_second):
    low = lax.broadcasted_iota(i32, (8, 128), 0) < 4
    first = partial_first + pltpu.roll(partial_first, 4, 0)
    second = partial_second + pltpu.roll(partial_second, 4, 0)
    return jnp.where(low, first, second)


def density_kernel(
    parts, coord, source, pos, mass, count, table, list_f, count_f, sums,
    list_v, count_v, list_s, count_s, order, rows, columns, total, natural, sem,
):
    table[...] = picked(parts[...], source[0:1, :])
    build_lists(table, coord, list_v, list_f, count_v, count_f)
    first_copy = pltpu.make_async_copy(list_v, list_s, sem.at[0])
    second_copy = pltpu.make_async_copy(count_v, count_s, sem.at[1])
    first_copy.start()
    second_copy.start()
    place = coord[...].astype(f32)
    for c in range(3):
        store_rows(rows, c, table[8 * c : 8 * c + 8, :] + place[c : c + 1, :])
    smooth = table[32:40, :]
    home = lax.broadcasted_iota(i32, (8, LANES), 1) < EXT
    safe = jnp.where(home, smooth, 1.0)
    store_rows(rows, 3, 1.0 / safe)
    for c in range(3):
        natural[c] = pos[c].reshape(CELLS, 256)
    natural[3] = live_mass(mass[...].reshape(CELLS, 256), count[...])

    def fill(block, _):
        start = pl.ds(pl.multiple_of(block * 8, 8), 8)
        cell = block * 8 + lax.broadcasted_iota(i32, (8, 256), 0)
        for c, value in enumerate((cell // 16, (cell // 4) % 4, cell % 4)):
            store_columns(columns, c, block, natural[c, start, :] + value.astype(f32))
        store_columns(columns, 3, block, natural[3, start, :])
        return 0

    lax.fori_loop(0, CELLS // 8, fill, 0)
    columns[NONE] = jnp.zeros((4, 8, 128), f32)
    total[...] = jnp.zeros_like(total)
    first_copy.wait()
    second_copy.wait()
    lane_index = lax.broadcasted_iota(i32, (8, 128), 1)

    def item(tile, lane, cells):
        at = lane_of(lane)
        row = [jnp.take_along_axis(rows[f, tile], at, axis=1) for f in range(4)]
        acc = None
        for cell in cells:
            d = [row[c] - columns[cell, c] for c in range(3)]
            r2 = d[0] * d[0] + d[1] * d[1] + d[2] * d[2]
            r = r2 * lax.rsqrt(jnp.maximum(r2, 1e-30))
            u = jnp.maximum(2.0 - r * row[3], 0.0)
            v = jnp.maximum(u - 1.0, 0.0)
            term = columns[cell, 3] * (u * u * u - 4.0 * (v * v * v))
            acc = term if acc is None else acc + term
        summed = jnp.sum(acc, axis=1, keepdims=True)
        total[tile] = total[tile] + jnp.where(lane_index == lane, summed, 0.0)

    run_items(work_items(count_s, order), BATCH_D, order, list_s, item)
    scale = 1.0 / (4.0 * math.pi * safe * safe * safe)
    for t in range(TILES):
        both = folded(total[t], total[TILES + t])
        sums[:, 128 * t : 128 * t + 128] = both * scale[:, 128 * t : 128 * t + 128]


def home_lanes():
    cell = np.arange(CELLS)
    lane = ((cell // 16 + 1) * EY + (cell // 4) % 4 + 1) * EZ + cell % 4 + 1
    return np.tile(lane.astype(np.int32), (8, 1))


def state(entropy, density):
    pressure = entropy * jnp.exp(jnp.log(density) * (-1.0 / 3.0))
    return pressure, jnp.sqrt(ADIABATIC * pressure * density)


def force_kernel(
    table, fresh, list_s, count_s, coord, home, pos, vel, mass, smooth, entropy, stored, count,
    active, sums, density, order, rows, columns, total, natural,
):
    is_cell = lax.broadcasted_iota(i32, (8, LANES), 1) < EXT
    live = lax.broadcasted_iota(i32, (8, LANES), 0).astype(f32) < table[LIVE : LIVE + 1, :]
    place = coord[...].astype(f32)

    def field(f):
        return table[8 * f : 8 * f + 8, :]

    rho = jnp.where(is_cell, jnp.where(live, fresh[...], field(9)), 1.0)
    row_h = jnp.where(is_cell, field(4), 1.0)
    row_p, row_s = state(field(8), rho)

    def features(h, sound, dens, pressure):
        a = math.sqrt(0.75 / math.pi) / (h * h)
        return 2.0 * a, a / h, 0.05 * h, 0.5 * sound, 2.0 * dens, pressure

    for c in range(3):
        store_rows(rows, c, field(c) + place[c : c + 1, :])
        store_rows(rows, 3 + c, 20.0 * field(5 + c))
    for f, value in enumerate(features(row_h, row_s, rho, row_p)):
        store_rows(rows, 6 + f, value)

    slot = lax.broadcasted_iota(i32, (CELLS, 128), 1)
    updated = lanes_to_cells(picked(rho, home[0:1, :]))
    old = stored[...].reshape(CELLS, 256)
    new = jnp.concatenate([jnp.where(slot < active[...], updated, old[:, :128]), old[:, 128:]], 1)
    density[...] = new.reshape(BX, BY, BZ, 256)
    for c in range(3):
        natural[c] = pos[c].reshape(CELLS, 256)
        natural[3 + c] = vel[c].reshape(CELLS, 256)
    natural[6] = live_mass(mass[...].reshape(CELLS, 256), count[...])
    natural[7] = smooth[...].reshape(CELLS, 256)
    natural[8] = entropy[...].reshape(CELLS, 256)
    natural[9] = new

    def fill(block, _):
        start = pl.ds(pl.multiple_of(block * 8, 8), 8)
        cell = block * 8 + lax.broadcasted_iota(i32, (8, 256), 0)
        for c, value in enumerate((cell // 16, (cell // 4) % 4, cell % 4)):
            store_columns(columns, c, block, natural[c, start, :] + value.astype(f32))
            store_columns(columns, 3 + c, block, 20.0 * natural[3 + c, start, :])
        dens = natural[9, start, :]
        pressure, sound = state(natural[8, start, :], dens)
        for f, value in enumerate(features(natural[7, start, :], sound, dens, pressure)):
            store_columns(columns, 6 + f, block, value)
        store_columns(columns, 12, block, natural[6, start, :])
        return 0

    lax.fori_loop(0, CELLS // 8, fill, 0)
    columns[NONE] = jnp.ones((13, 8, 128), f32)
    columns[NONE, 12] = jnp.zeros((8, 128), f32)
    total[...] = jnp.zeros_like(total)
    lane_index = lax.broadcasted_iota(i32, (8, 128), 1)

    def item(tile, lane, cells):
        at = lane_of(lane)
        row = [jnp.take_along_axis(rows[f, tile], at, axis=1) for f in range(12)]
        acc = [None] * 3
        for cell in cells:
            col = [columns[cell, f] for f in range(13)]
            d = [row[c] - col[c] for c in range(3)]
            r2 = d[0] * d[0] + d[1] * d[1] + d[2] * d[2]
            closing = (
                (row[3] - col[3]) * d[0] + (row[4] - col[4]) * d[1] + (row[5] - col[5]) * d[2]
            )
            inverse = lax.rsqrt(jnp.maximum(r2, 1e-30))
            r = r2 * inverse

            def slope(twice, per):
                t = per * r
                u = jnp.maximum(twice - t, 0.0)
                s = jnp.minimum(t, u)
                return s * (u + (u - s))

            h = row[8] + col[8]
            approach = (h * jnp.minimum(closing, 0.0)) * pl.reciprocal(r2 + h * h, approx=True)
            viscosity = (approach * (approach - (row[9] + col[9]))) * pl.reciprocal(
                row[10] + col[10], approx=True
            )
            weight = (row[11] + viscosity) * slope(row[6], row[7])
            weight = weight + (col[11] + viscosity) * slope(col[6], col[7])
            weight = weight * (inverse * col[12])
            for c in range(3):
                term = weight * d[c]
                acc[c] = term if acc[c] is None else acc[c] + term
        mine = lane_index == lane
        for c in range(3):
            summed = jnp.sum(acc[c], axis=1, keepdims=True)
            total[c, tile] = total[c, tile] + jnp.where(mine, summed, 0.0)

    run_items(work_items(count_s, order), BATCH_F, order, list_s, item)
    for c in range(3):
        for t in range(TILES):
            sums[8 * c : 8 * c + 8, 128 * t : 128 * t + 128] = folded(total[c, t], total[c, TILES + t])


def spread_kernel(pushed, home, active, out):
    mine = picked(pushed[...], home[0:1, :])
    slot = lax.broadcasted_iota(i32, (CELLS, 128), 1)
    for c in range(3):
        rows = lanes_to_cells(mine[8 * c : 8 * c + 8, :])
        rows = jnp.where(slot < active[...], rows, 0.0)
        out[c] = jnp.concatenate([rows, jnp.zeros((CELLS, 128), f32)], 1).reshape(BX, BY, BZ, 256)


VMEM_SPEC = pl.BlockSpec(memory_space=pltpu.VMEM)
SMEM_SPEC = pl.BlockSpec(memory_space=pltpu.SMEM)
PARAMS = pltpu.CompilerParams(vmem_limit_bytes=56 * 1024 * 1024)


def shape(*dims, dtype=f32):
    return jax.ShapeDtypeStruct(dims, dtype)


def call(kernel, inputs, outputs, in_specs=None, scratch=()):
    single = not isinstance(outputs, (list, tuple))
    return pl.pallas_call(
        kernel,
        out_shape=outputs,
        in_specs=in_specs or [VMEM_SPEC] * len(inputs),
        out_specs=VMEM_SPEC if single else [VMEM_SPEC] * len(outputs),
        scratch_shapes=list(scratch),
        compiler_params=PARAMS,
    )(*inputs)


def ring(axis, by):
    devices = lax.axis_size(axis)
    return [(i, (i + by) % devices) for i in range(devices)]


def first_exchange(table, faces):
    y_part, z_part, edge = faces[:, :128], faces[:, 128:256], faces[:, 256:320]
    across = ("gy", "gz")
    y_in = lax.ppermute(y_part, across, [(0, 2), (1, 3), (2, 0), (3, 1)])
    z_in = lax.ppermute(z_part, across, [(0, 1), (1, 0), (2, 3), (3, 2)])
    edge_in = lax.ppermute(edge, across, [(0, 3), (1, 2), (2, 1), (3, 0)])
    low = jnp.concatenate([table[:, :16], y_in[:, :8], z_in[:, :8], edge_in[:, :4]], 1)
    high = jnp.concatenate([table[:, 240:], y_in[:, 120:], z_in[:, 120:], edge_in[:, 60:]], 1)
    before = lax.ppermute(high, "gx", ring("gx", 1))
    after = lax.ppermute(low, "gx", ring("gx", -1))
    unused = jnp.zeros((ROWS, LANES - EXT), f32)
    return jnp.concatenate([table, y_in, z_in, edge_in, before, after, unused], 1)


def turned(values, by):
    return jnp.concatenate([values[:, -by:], values[:, :-by]], 1) if by > 0 else jnp.concatenate(
        [values[:, -by:], values[:, :-by]], 1
    )


def shared_sums(sums, coord):
    plane = EY * EZ
    top = BX * plane
    before = lax.ppermute(sums[:, top : top + 2 * plane], "gx", ring("gx", 1))
    after = lax.ppermute(sums[:, : 2 * plane], "gx", ring("gx", -1))
    middle = sums[:, 2 * plane : top]
    sums = jnp.concatenate(
        [sums[:, : 2 * plane] + before, middle, sums[:, top:EXT] + after, sums[:, EXT:]], 1
    )
    for axis, step, position, extent in (("gy", EZ, coord[1:2], BY), ("gz", 1, coord[2:3], BZ)):
        other = lax.ppermute(sums, axis, ring(axis, 1))
        shift = extent * step
        low = (position == -1) | (position == 0)
        high = (position == extent - 1) | (position == extent)
        sums = sums + jnp.where(low, turned(other, -shift), jnp.where(high, turned(other, shift), 0.0))
    return sums


def returned_sums(sums, coord):
    plane = EY * EZ
    top = BX * plane
    before = lax.ppermute(sums[:, top + plane : EXT], "gx", ring("gx", 1))
    after = lax.ppermute(sums[:, :plane], "gx", ring("gx", -1))
    sums = jnp.concatenate(
        [
            sums[:, :plane],
            sums[:, plane : 2 * plane] + before,
            sums[:, 2 * plane : top],
            sums[:, top : top + plane] + after,
            sums[:, top + plane :],
        ],
        1,
    )
    for axis, step, position, extent in (("gy", EZ, coord[1:2], BY), ("gz", 1, coord[2:3], BZ)):
        other = lax.ppermute(sums, axis, ring(axis, 1))
        shift = extent * step
        sums = sums + jnp.where(
            position == 0,
            turned(other, -shift),
            jnp.where(position == extent - 1, turned(other, shift), 0.0),
        )
    return sums


def shards(pos, vel, mass, smooth, entropy, stored, particle_count, active_count, pair_side):
    coord_np, source_np = maps()
    coord, source = jnp.asarray(coord_np), jnp.asarray(source_np)
    home = jnp.asarray(home_lanes())
    count = particle_count.reshape(CELLS, 1)
    active = active_count.reshape(CELLS, 1)
    flags = jnp.concatenate(
        [
            pair_side.reshape(26, CELLS).astype(f32),
            active_count.reshape(1, CELLS).astype(f32),
            jnp.zeros((ROWS - FLAGS - 27, CELLS), f32),
        ],
        0,
    )
    inputs = (pos, vel, mass, smooth, entropy, stored, count, flags, jnp.asarray(sent_cells()))
    table, faces = call(pack_kernel, inputs, [shape(ROWS, CELLS), shape(ROWS, 384)])
    parts = first_exchange(table, faces)
    inputs = (parts, coord, source, pos, mass, count)
    table, list_f, count_f, sums = call(
        density_kernel,
        inputs,
        [
            shape(ROWS, LANES), shape(28, GROUPS, dtype=i32), shape(1, GROUPS, dtype=i32),
            shape(ACT, LANES),
        ],
        scratch=[
            pltpu.VMEM((28, GROUPS), i32), pltpu.VMEM((1, GROUPS), i32),
            pltpu.SMEM((28, GROUPS), i32), pltpu.SMEM((1, GROUPS), i32),
            pltpu.SMEM((GROUPS + 128,), i32), pltpu.VMEM((4, 2 * TILES, 8, 128), f32),
            pltpu.VMEM((CELLS + 1, 4, 8, 128), f32), pltpu.VMEM((2 * TILES, 8, 128), f32),
            pltpu.VMEM((4, CELLS, 256), f32), pltpu.SemaphoreType.DMA((2,)),
        ],
    )
    fresh = shared_sums(sums, coord)
    inputs = (
        table, fresh, list_f, count_f, coord, home, pos, vel, mass, smooth, entropy, stored,
        count, active,
    )
    sums, density = call(
        force_kernel,
        inputs,
        [shape(24, LANES), shape(BX, BY, BZ, 256)],
        in_specs=[VMEM_SPEC, VMEM_SPEC, SMEM_SPEC, SMEM_SPEC] + [VMEM_SPEC] * 10,
        scratch=[
            pltpu.SMEM((GROUPS + 128,), i32), pltpu.VMEM((12, 2 * TILES, 8, 128), f32),
            pltpu.VMEM((CELLS + 1, 13, 8, 128), f32), pltpu.VMEM((3, 2 * TILES, 8, 128), f32),
            pltpu.VMEM((10, CELLS, 256), f32),
        ],
    )
    pushed = returned_sums(sums, coord)
    acceleration = call(spread_kernel, (pushed, home, active), shape(3, BX, BY, BZ, 256))
    return density, acceleration


def solution(mesh):
    cells = P("gx", "gy", "gz", None)
    vectors = P(None, "gx", "gy", "gz", None)
    counts = P("gx", "gy", "gz")
    in_specs = (
        vectors, vectors, cells, cells, cells, cells, counts, counts, P(None, "gx", "gy", "gz"),
    )
    return jax.shard_map(
        shards, mesh=mesh, in_specs=in_specs, out_specs=(cells, vectors), check_vma=False
    )
```

profile of v0, /device:TPU:0, one launch (start us, length us, event | category | flops | bytes accessed | tf_op | source)
XLA Modules:
  0.0 441.3 jit_solution(17675087951618955119)
XLA Ops:
  3.3 3.9 shard_map.140
  7.2 0.9 fusion.4
  8.1 1.7 collective-permute-start.1
  9.7 2.7 collective-permute-start
  12.5 0.8 slice.124
  13.8 4.9 %collective-permute-done.2 = f32[112,64]{1,0:T(8,128)S(1)} collective-permute-done((f32[112,64]{1,0:T(8,128)S(1)}, f32[112,64]{1,0:T(8,128)S(1)}, u32[]{:S(2)}, u32[]{:S(2)}) %collective-permute-start.2) | collective-permute-done | bytes 28704 | tf_op jit(solution)/shard_map/ppermute | solution.py:475
  19.0 4.3 collective-permute-start.4
  23.5 1.6 collective-permute-done.4
  25.2 5.3 %collective-permute-done.3 = f32[112,36]{1,0:T(8,128)S(1)} collective-permute-done((f32[112,36]{1,0:T(8,128)S(1)}, f32[112,36]{1,0:T(8,128)S(1)}, u32[]{:S(2)}, u32[]{:S(2)}) %collective-permute-start.3) | collective-permute-done | bytes 16160 | tf_op jit(solution)/shard_map/ppermute | solution.py:478
  30.4 0.8 concatenate.45.parts
  31.3 113.1 %shard_map.141 = (f32[112,768]{1,0:T(8,128)}, s32[28,1536]{1,0:T(8,128)}, s32[1,1536]{1,0:T(1,128)}, f32[8,768]{1,0:T(8,128)}) custom-call(f32[112,768]{1,0:T(8,128)} %concatenate.45.parts, s32[8,768]{1,0:T(8,128)} %constant.7.clone.coord, s32[8,768]{1,0:T(8,128)} %constant.8.clone.source, f32[3,16,4,4,256]{4,3,2,1,0:T(4,128)} %pos.5, ...), custom_call_target="tpu_custom_call" | custom-call | tf_op jit(solution)/shard_map/pallas_call | solution.py:455
  144.4 0.8 fusion.17
  145.2 5.1 %collective-permute-start.6 = (f32[8,72]{1,0:T(8,128)S(1)}, f32[8,72]{1,0:T(8,128)S(1)}, u32[]{:S(2)}, u32[]{:S(2)}) collective-permute-start(f32[8,72]{1,0:T(8,128)S(1)} %get-tuple-element.49), channel_id=1, source_target_pairs={{0,124},{4,0},{8,4},{12,8},{16,12},{20,16},{24,20},{28,24},{32,28}... | collective-permute-start | bytes 6920 | tf_op jit(solution)/shard_map/ppermute | solution.py:494
  151.8 5.3 %collective-permute-done.7 = f32[8,768]{1,0:T(8,128)S(1)} collective-permute-done((f32[8,768]{1,0:T(8,128)S(1)}, f32[8,768]{1,0:T(8,128)S(1)}, u32[]{:S(2)}, u32[]{:S(2)}) %collective-permute-start.7) | collective-permute-done | bytes 24608 | tf_op jit(solution)/shard_map/ppermute | solution.py:500
  159.5 2.4 collective-permute-done.8
  163.5 245.9 %shard_map.142 = (f32[24,768]{1,0:T(8,128)}, f32[16,4,4,256]{3,2,1,0:T(4,128)}) custom-call(f32[112,768]{1,0:T(8,128)} %get-tuple-element.12.table, f32[8,768]{1,0:T(8,128)} %fusion.3.fresh, s32[28,1536]{1,0:T(8,128)} %get-tuple-element.14.list_s, s32[1,1536]{1,0:T(1,128)} %get-tuple-element.15.count_s, s32[8,768]{1,0:T(8,128)} %constant.7.clone.coord, ...), custom_call_target="tpu_custom_call" | custom-call | tf_op jit(solution)/shard_map/pallas_call | solution.py:455
  410.2 2.3 collective-permute-start.10
  412.5 1.4 collective-permute-done.10
  413.9 0.9 slice_add_fusion
  414.9 6.3 %collective-permute-done.9 = f32[24,36]{1,0:T(8,128)S(1)} collective-permute-done((f32[24,36]{1,0:T(8,128)S(1)}, f32[24,36]{1,0:T(8,128)S(1)}, u32[]{:S(2)}, u32[]{:S(2)}) %collective-permute-start.9) | collective-permute-done | bytes 3488 | tf_op jit(solution)/shard_map/ppermute | solution.py:511
  421.5 5.8 %collective-permute-done.11 = f32[24,768]{1,0:T(8,128)S(1)} collective-permute-done((f32[24,768]{1,0:T(8,128)S(1)}, f32[24,768]{1,0:T(8,128)S(1)}, u32[]{:S(2)}, u32[]{:S(2)}) %collective-permute-start.11) | collective-permute-done | bytes 73760 | tf_op jit(solution)/shard_map/ppermute | solution.py:524
  428.3 5.7 %collective-permute-start.12 = (f32[24,768]{1,0:T(8,128)S(1)}, f32[24,768]{1,0:T(8,128)S(1)}, u32[]{:S(2)}, u32[]{:S(2)}) collective-permute-start(f32[24,768]{1,0:T(8,128)S(1)} %fusion), channel_id=1, source_target_pairs={{0,1},{1,0},{2,3},{3,2},{4,5},{5,4},{6,7},{7,6},{8,9},{9,8},{10,11... | collective-permute-start | bytes 221192 | tf_op jit(solution)/shard_map/ppermute | solution.py:524
  434.0 2.3 collective-permute-done.12
  437.9 3.4 shard_map.143
  (79 shorter events, 12.8 us)
Async XLA Ops:
  0.6 0.9 copy-start.5
  1.3 1.1 copy-start.2
  8.1 5.6 %copy-start = (f32[112,256]{1,0:T(8,128)S(1)}, f32[112,256]{1,0:T(8,128)}, u32[]{:S(2)}) copy-start(f32[112,256]{1,0:T(8,128)} %get-tuple-element.10) | copy-start | bytes 344068
  8.1 10.8 %collective-permute-start.1 = (f32[112,128]{1,0:T(8,128)S(1)}, f32[112,128]{1,0:T(8,128)S(1)}, u32[]{:S(2)}, u32[]{:S(2)}) collective-permute-start(f32[112,128]{1,0:T(8,128)S(1)} %get-tuple-element.18), channel_id=1, source_target_pairs={{0,1},{1,0},{2,3},{3,2},{4,5},{5,4},{6,7},{7,6},{8,9},{9,8},{10,11... | collective-permute-start | bytes 172040 | tf_op jit(solution)/shard_map/ppermute | solution.py:474
  9.7 9.0 %collective-permute-start = (f32[112,128]{1,0:T(8,128)S(1)}, f32[112,128]{1,0:T(8,128)S(1)}, u32[]{:S(2)}, u32[]{:S(2)}) collective-permute-start(f32[112,128]{1,0:T(8,128)S(1)} %get-tuple-element.19), channel_id=1, source_target_pairs={{0,2},{1,3},{2,0},{3,1},{4,6},{5,7},{6,4},{7,5},{8,10},{9,11},{10,... | collective-permute-start | bytes 172040 | tf_op jit(solution)/shard_map/ppermute | solution.py:473
  13.3 5.4 %collective-permute-start.2 = (f32[112,64]{1,0:T(8,128)S(1)}, f32[112,64]{1,0:T(8,128)S(1)}, u32[]{:S(2)}, u32[]{:S(2)}) collective-permute-start(f32[112,64]{1,0:T(8,128)S(1)} %slice.124), channel_id=1, source_target_pairs={{0,3},{1,2},{2,1},{3,0},{4,7},{5,6},{6,5},{7,4},{8,11},{9,10},{10,... | collective-permute-start | bytes 86024 | tf_op jit(solution)/shard_map/ppermute | solution.py:475
  19.0 6.1 %collective-permute-start.4 = (f32[112,36]{1,0:T(8,128)S(1)}, f32[112,36]{1,0:T(8,128)S(1)}, u32[]{:S(2)}, u32[]{:S(2)}) collective-permute-start(f32[112,36]{1,0:T(8,128)S(1)} %pad_maximum_fusion.1), channel_id=1, source_target_pairs={{0,124},{4,0},{8,4},{12,8},{16,12},{20,16},{24,20},{28,24},{32,28}... | collective-permute-start | bytes 48392 | tf_op jit(solution)/shard_map/ppermute | solution.py:479
  23.5 7.0 %collective-permute-start.3 = (f32[112,36]{1,0:T(8,128)S(1)}, f32[112,36]{1,0:T(8,128)S(1)}, u32[]{:S(2)}, u32[]{:S(2)}) collective-permute-start(f32[112,36]{1,0:T(8,128)S(1)} %pad_maximum_fusion), channel_id=1, source_target_pairs={{0,4},{4,8},{8,12},{12,16},{16,20},{20,24},{24,28},{28,32},{32,36}... | collective-permute-start | bytes 48392 | tf_op jit(solution)/shard_map/ppermute | solution.py:478
  144.4 6.7 %copy-start.3 = (f32[8,768]{1,0:T(8,128)S(1)}, f32[8,768]{1,0:T(8,128)}, u32[]{:S(2)}) copy-start(f32[8,768]{1,0:T(8,128)} %get-tuple-element.13) | copy-start | bytes 73732
  145.2 6.4 %collective-permute-start.5 = (f32[8,72]{1,0:T(8,128)S(1)}, f32[8,72]{1,0:T(8,128)S(1)}, u32[]{:S(2)}, u32[]{:S(2)}) collective-permute-start(f32[8,72]{1,0:T(8,128)S(1)} %get-tuple-element.48), channel_id=1, source_target_pairs={{0,4},{4,8},{8,12},{12,16},{16,20},{20,24},{24,28},{28,32},{32,36}... | collective-permute-start | bytes 6920 | tf_op jit(solution)/shard_map/ppermute | solution.py:493
  145.2 6.4 %collective-permute-start.6 = (f32[8,72]{1,0:T(8,128)S(1)}, f32[8,72]{1,0:T(8,128)S(1)}, u32[]{:S(2)}, u32[]{:S(2)}) collective-permute-start(f32[8,72]{1,0:T(8,128)S(1)} %get-tuple-element.49), channel_id=1, source_target_pairs={{0,124},{4,0},{8,4},{12,8},{16,12},{20,16},{24,20},{28,24},{32,28}... | collective-permute-start | bytes 6920 | tf_op jit(solution)/shard_map/ppermute | solution.py:494
  151.8 5.4 %collective-permute-start.7 = (f32[8,768]{1,0:T(8,128)S(1)}, f32[8,768]{1,0:T(8,128)S(1)}, u32[]{:S(2)}, u32[]{:S(2)}) collective-permute-start(f32[8,768]{1,0:T(8,128)S(1)} %pad_maximum_fusion.2), channel_id=1, source_target_pairs={{0,2},{2,0},{1,3},{3,1},{4,6},{6,4},{5,7},{7,5},{8,10},{10,8},{9,1... | collective-permute-start | bytes 73736 | tf_op jit(solution)/shard_map/ppermute | solution.py:500
  157.3 0.7 copy-start.12
  157.9 0.7 copy-start.4
  158.0 3.9 collective-permute-start.8
  162.1 0.7 copy-start.10
  409.4 5.4 %copy-start.1 = (f32[24,768]{1,0:T(8,128)S(1)}, f32[24,768]{1,0:T(8,128)}, u32[]{:S(2)}) copy-start(f32[24,768]{1,0:T(8,128)} %get-tuple-element.17) | copy-start | bytes 221188
  410.2 3.7 collective-permute-start.10
  414.8 6.4 %collective-permute-start.9 = (f32[24,36]{1,0:T(8,128)S(1)}, f32[24,36]{1,0:T(8,128)S(1)}, u32[]{:S(2)}, u32[]{:S(2)}) collective-permute-start(f32[24,36]{1,0:T(8,128)S(1)} %get-tuple-element.31), channel_id=1, source_target_pairs={{0,4},{4,8},{8,12},{12,16},{16,20},{20,24},{24,28},{28,32},{32,36}... | collective-permute-start | bytes 10376 | tf_op jit(solution)/shard_map/ppermute | solution.py:511
  421.4 5.9 %collective-permute-start.11 = (f32[24,768]{1,0:T(8,128)S(1)}, f32[24,768]{1,0:T(8,128)S(1)}, u32[]{:S(2)}, u32[]{:S(2)}) collective-permute-start(f32[24,768]{1,0:T(8,128)S(1)} %concatenate.51), channel_id=1, source_target_pairs={{0,2},{2,0},{1,3},{3,1},{4,6},{6,4},{5,7},{7,5},{8,10},{10,8},{9,1... | collective-permute-start | bytes 221192 | tf_op jit(solution)/shard_map/ppermute | solution.py:524
  427.4 0.7 copy-start.9
  427.5 0.7 copy-start.8
  428.3 8.0 %collective-permute-start.12 = (f32[24,768]{1,0:T(8,128)S(1)}, f32[24,768]{1,0:T(8,128)S(1)}, u32[]{:S(2)}, u32[]{:S(2)}) collective-permute-start(f32[24,768]{1,0:T(8,128)S(1)} %fusion), channel_id=1, source_target_pairs={{0,1},{1,0},{2,3},{3,2},{4,5},{5,4},{6,7},{7,6},{8,9},{9,8},{10,11... | collective-permute-start | bytes 221192 | tf_op jit(solution)/shard_map/ppermute | solution.py:524
  436.5 0.7 copy-start.6
  (3 other events, 2.0 us)
where the time goes:
time: 437 us; the launch traced here: 441 us
  Pallas kernels  366 us (84%)
  waiting for transfers between devices  35.9 us (8%)
  starting transfers between devices  22.4 us (5%)
  local copies, waits for them, and re-layouts  11.5 us (3%)
    pallas_call x4, Pallas kernels, call(): pl.pallas_call(kernel, out_shape=outputs, in_specs=in_specs or [VMEM_SPEC...  366 us
  transfers between devices with their start and end apart: 13, of which 10 were waited for; matrix products, arithmetic and copies ran while one was open for 1% of the time, Pallas kernels for 0%

commit v1 on v0

--- a/solution.py
+++ b/solution.py
@@ -20,9 +20,13 @@
 ROWS = 112
 FLAGS = 80
 LIVE = 106
-SPAN = 4
-BATCH_D = 4
-BATCH_F = 2
+SPAN = 3
+WORDS = 9
+ITEM_ROWS = 96
+LIST_ROWS = 112
+HELD = 16
+BATCH_D = 8
+BATCH_F = 4
 NONE = CELLS
 ADIABATIC = 5.0 / 3.0
 HIGHEST = lax.Precision.HIGHEST
@@ -126,25 +130,39 @@
     faces[...] = picked(table[...], sent[0:1, :])
 
 
-def doubled(rows, group):
-    swapped = pltpu.roll(rows, 4, 0)
-    low = lax.broadcasted_iota(i32, rows.shape, 0) < 4
-    return jnp.where(low, rows, swapped) if group == 0 else jnp.where(low, swapped, rows)
+def segment_units():
+    row = lax.broadcasted_iota(i32, (24, 256), 0) % 8
+    lane = lax.broadcasted_iota(i32, (24, 256), 1)
+    return (row == lane // 128 * 4 + lane % 128 // 32).astype(f32)
 
 
 def store_rows(target, feature, rows):
+    high = rows.astype(jnp.bfloat16).astype(f32)
+    rest = rows - high
+    middle = rest.astype(jnp.bfloat16).astype(f32)
+    parts = jnp.concatenate([high, middle, rest - middle], 0)
+    spread = lax.dot_general(
+        parts, segment_units(), (((0,), (0,)), ((), ())), preferred_element_type=f32
+    )
     for group in range(2):
-        both = doubled(rows, group)
-        for t in range(TILES):
-            target[feature, group * TILES + t] = both[:, 128 * t : 128 * t + 128]
-
-
-def store_columns(target, feature, block, natural):
-    low = lax.broadcasted_iota(i32, (8, 128), 0) < 4
-    for s in range(8):
-        first = jnp.broadcast_to(natural[s : s + 1, :128], (8, 128))
-        second = jnp.broadcast_to(natural[s : s + 1, 128:], (8, 128))
-        target[block * 8 + s, feature] = jnp.where(low, first, second)
+        for block in range(LANES // 8):
+            at = (group * LANES + block * 8) * HELD + feature
+            target[pl.ds(at, 8, stride=HELD), :] = spread[
+                8 * block : 8 * block + 8, 128 * group : 128 * group + 128
+            ]
+
+
+def store_columns(target, feature, block, count, natural):
+    part = lax.broadcasted_iota(i32, (8, 128), 1) // 32
+    for half in range(2):
+        slots = natural[:, 128 * half : 128 * half + 128]
+        turns = [slots] + [pltpu.roll(slots, 32 * t, 1) for t in range(1, 4)]
+        for k in range(4):
+            value = turns[(0 - k) % 4]
+            for r in range(1, 4):
+                value = jnp.where(part == r, turns[(r - k) % 4], value)
+            at = (block * 8 * count + feature) * 8 + half * 4 + k
+            target.reshape((CELLS + 1) * count * 8, 128)[pl.ds(at, 8, stride=count * 8), :] = value
 
 
 def build_lists(table, coord, list_d, list_f, count_d, count_f):
@@ -202,78 +220,137 @@
                     e = jnp.where(moves[p + step], entries[p + step], e)
                 moved.append(e)
             entries = moved
-        entries = [e & 1023 for e in entries] + [jnp.full((2, LANES), NONE, i32)]
-        for p in range(28):
+        entries = [e & 1023 for e in entries]
+        for p in range(WORDS):
+            word = entries[3 * p] + (entries[3 * p + 1] << 10) + (entries[3 * p + 2] << 20)
             for group in range(2):
-                target[p : p + 1, group * LANES : group * LANES + LANES] = entries[p][group : group + 1]
+                for t in range(TILES):
+                    at = (p * 2 + group) * TILES + t
+                    target[at : at + 1, :] = word[group : group + 1, 128 * t : 128 * t + 128]
+        target[WORDS * 2 * TILES :, :] = jnp.full((LIST_ROWS - WORDS * 2 * TILES, 128), NONE, i32)
         for group in range(2):
-            counted[0:1, group * LANES : group * LANES + LANES] = kept[group : group + 1]
-
-
-def work_items(counts, order):
-    def step(i, carry):
-        at, total = carry
-        for u in range(16):
-            group = i * 16 + u
-            items = (counts[0, group] + SPAN - 1) // SPAN
-            order[at] = group + items * 65536
-            at = at + (items > 0).astype(i32)
-            total = total + items
-        return at, total
-
-    at, total = lax.fori_loop(0, GROUPS // 16, step, (jnp.int32(0), jnp.int32(0)))
-    order[at] = (GROUPS - 1) + (1 << 30)
+            for t in range(TILES):
+                counted[group * TILES + t : group * TILES + t + 1, :] = kept[
+                    group : group + 1, 128 * t : 128 * t + 128
+                ]
+        counted[2 * TILES :, :] = jnp.zeros((16 - 2 * TILES, 128), i32)
+
+
+def work_items(counts, items_v, items_s, ends, ends_v, ends_s, sem):
+    items = jnp.floor((counts[...] + SPAN - 1).astype(f32) * (1.00002 / SPAN))
+    row = lax.broadcasted_iota(i32, (128, 128), 0)
+    lane = lax.broadcasted_iota(i32, (128, 128), 1)
+    within = jnp.dot(items, (row <= lane).astype(f32), preferred_element_type=f32)
+    whole = jnp.broadcast_to(within[:, 127:128], (16, 128))
+    earlier = (
+        lax.broadcasted_iota(i32, (16, 16), 1) < lax.broadcasted_iota(i32, (16, 16), 0)
+    ).astype(f32)
+    end = within + jnp.dot(earlier, whole, precision=HIGHEST, preferred_element_type=f32)
+    ends_v[...] = end
+    copy = pltpu.make_async_copy(ends_v, ends_s, sem)
+    copy.start()
+    for t in range(2 * TILES):
+        ends[128 * t : 128 * t + 128, :] = jnp.broadcast_to(end[t : t + 1, :], (128, 128)).T
+    items_v[...] = jnp.full((ITEM_ROWS, 128), (GROUPS - 1) * 2049, i32)
+    copy.wait()
+    last = [ends_s[t, 127].astype(i32) for t in range(2 * TILES)]
+    total = last[-1]
+    lanes = lax.broadcasted_iota(i32, (8, 128), 1)
+
+    def fill(j, _):
+        first = j * 128
+        index = first + lanes
+        number = index.astype(f32)
+        begin = jnp.int32(0)
+        stop = jnp.int32(0)
+        before = jnp.int32(0)
+        for e in last:
+            begin = begin + (e <= first).astype(i32)
+            stop = stop + (e <= first + 127).astype(i32)
+            before = jnp.where(e <= first, e, before)
+        stop = jnp.minimum(stop + 1, 2 * TILES)
+
+        def tile(t, carry):
+            passed, start = carry
+            for u in range(16):
+                e = ends[pl.ds(pl.multiple_of(t * 128 + u * 8, 8), 8), :]
+                over = e <= number
+                passed = passed + jnp.where(over, 1.0, 0.0)
+                start = jnp.maximum(start, jnp.where(over, e, 0.0))
+            return passed, start
+
+        zero = jnp.zeros((8, 128), f32)
+        passed, start = lax.fori_loop(begin, stop, tile, (zero, zero))
+        group = begin * 128 + jnp.sum(passed, 0, keepdims=True).astype(i32)
+        start = jnp.maximum(jnp.max(start, 0, keepdims=True).astype(i32), before)
+        code = group + ((index[0:1] - start) * GROUPS + group) * 2048
+        items_v[pl.ds(j, 1), :] = jnp.where(index[0:1] < total, code, (GROUPS - 1) * 2049)
+        return 0
+
+    lax.fori_loop(0, (total + 127) >> 7, fill, 0)
+    copy = pltpu.make_async_copy(items_v, items_s, sem)
+    copy.start()
+    copy.wait()
     return total
 
 
-def run_items(total, batch, order, lists, item):
-    def advance(at, done):
-        entry = order[at]
-        last = done + 1 >= (entry >> 16)
-        return (entry & 65535) + done * 65536, jnp.where(last, at + 1, at), jnp.where(last, 0, done + 1)
-
-    def take(at, done):
-        taken = []
-        for _ in range(batch):
-            code, at, done = advance(at, done)
-            taken.append(code)
-        return at, done, taken
-
-    at, done, first = take(jnp.int32(0), jnp.int32(0))
-
-    def step(_, carry):
-        at, done, codes = carry
-        at, done, later = take(at, done)
-        for code in codes:
-            group, part = code & 65535, code >> 16
-            cells = [lists[part * SPAN + v, group] for v in range(SPAN)]
-            item(group >> 7, group & 127, cells)
-        return at, done, later
-
-    lax.fori_loop(0, (total + batch - 1) // batch, step, (at, done, first))
-
-
-def lane_of(lane):
-    return jnp.full((8, 128), lane, i32)
-
-
-def folded(partial_first, partial_second):
-    low = lax.broadcasted_iota(i32, (8, 128), 0) < 4
-    first = partial_first + pltpu.roll(partial_first, 4, 0)
-    second = partial_second + pltpu.roll(partial_second, 4, 0)
-    return jnp.where(low, first, second)
+def run_items(total, batch, items, lists, item, add):
+    per_row = 128 // batch
+
+    def take(turn):
+        codes = [items[turn // per_row, (turn % per_row) * batch + u] for u in range(batch)]
+        return codes, [lists[code >> 18, (code >> 11) & 127] for code in codes]
+
+    def step(turn, carry):
+        codes, words = carry
+        later = take(turn + 1)
+        results = []
+        for code, word in zip(codes, words):
+            group = code & 2047
+            results.append((group, item(group, (word & 1023, (word >> 10) & 1023, word >> 20))))
+        for group, values in results:
+            add(group, values)
+        return later
+
+    lax.fori_loop(0, (total + batch - 1) // batch, step, take(jnp.int32(0)))
+
+
+def row_sums(tiles, part_index, count, reduced):
+    def block(i, _):
+        for u in range(4):
+            value = None
+            for s in range(8):
+                at = ((i * 32 + u * 8) * count + part_index) * 8 + s
+                part = tiles.reshape(GROUPS * count * 8, 128)[pl.ds(at, 8, stride=8 * count), :]
+                value = part if value is None else value + part
+            reduced[pl.ds(pl.multiple_of(i * 32 + u * 8, 8), 8), :] = value
+        return 0
+
+    lax.fori_loop(0, GROUPS // 32, block, 0)
+    row = lax.broadcasted_iota(i32, (8, 128), 0)
+    segment = lax.broadcasted_iota(i32, (8, 128), 1) // 32
+    out = None
+    for group in range(2):
+        values = reduced[LANES * group : LANES * group + LANES, :]
+        unit = (row == segment + 4 * group).astype(f32)
+        high = values.astype(jnp.bfloat16).astype(f32)
+        for part in (high, values - high):
+            term = lax.dot_general(
+                unit, part, (((1,), (1,)), ((), ())), preferred_element_type=f32
+            )
+            out = term if out is None else out + term
+    return out
 
 
 def density_kernel(
     parts, coord, source, pos, mass, count, table, list_f, count_f, sums,
-    list_v, count_v, list_s, count_s, order, rows, columns, total, natural, sem,
+    list_v, count_v, list_s, items_v, items_s, ends, ends_v, ends_s, rows, columns, total, reduced,
+    natural, sem,
 ):
     table[...] = picked(parts[...], source[0:1, :])
     build_lists(table, coord, list_v, list_f, count_v, count_f)
-    first_copy = pltpu.make_async_copy(list_v, list_s, sem.at[0])
-    second_copy = pltpu.make_async_copy(count_v, count_s, sem.at[1])
-    first_copy.start()
-    second_copy.start()
+    list_copy = pltpu.make_async_copy(list_v, list_s, sem.at[0])
+    list_copy.start()
     place = coord[...].astype(f32)
     for c in range(3):
         store_rows(rows, c, table[8 * c : 8 * c + 8, :] + place[c : c + 1, :])
@@ -289,37 +366,36 @@
         start = pl.ds(pl.multiple_of(block * 8, 8), 8)
         cell = block * 8 + lax.broadcasted_iota(i32, (8, 256), 0)
         for c, value in enumerate((cell // 16, (cell // 4) % 4, cell % 4)):
-            store_columns(columns, c, block, natural[c, start, :] + value.astype(f32))
-        store_columns(columns, 3, block, natural[3, start, :])
+            store_columns(columns, c, block, 4, natural[c, start, :] + value.astype(f32))
+        store_columns(columns, 3, block, 4, natural[3, start, :])
         return 0
 
     lax.fori_loop(0, CELLS // 8, fill, 0)
     columns[NONE] = jnp.zeros((4, 8, 128), f32)
     total[...] = jnp.zeros_like(total)
-    first_copy.wait()
-    second_copy.wait()
-    lane_index = lax.broadcasted_iota(i32, (8, 128), 1)
-
-    def item(tile, lane, cells):
-        at = lane_of(lane)
-        row = [jnp.take_along_axis(rows[f, tile], at, axis=1) for f in range(4)]
+    list_copy.wait()
+
+    def item(group, cells):
+        row = [rows[pl.ds(group * HELD + f, 8, stride=0), :] for f in range(4)]
         acc = None
         for cell in cells:
-            d = [row[c] - columns[cell, c] for c in range(3)]
+            col = [columns[cell, f] for f in range(4)]
+            d = [row[c] - col[c] for c in range(3)]
             r2 = d[0] * d[0] + d[1] * d[1] + d[2] * d[2]
             r = r2 * lax.rsqrt(jnp.maximum(r2, 1e-30))
             u = jnp.maximum(2.0 - r * row[3], 0.0)
             v = jnp.maximum(u - 1.0, 0.0)
-            term = columns[cell, 3] * (u * u * u - 4.0 * (v * v * v))
+            term = col[3] * (u * u * u - 4.0 * (v * v * v))
             acc = term if acc is None else acc + term
-        summed = jnp.sum(acc, axis=1, keepdims=True)
-        total[tile] = total[tile] + jnp.where(lane_index == lane, summed, 0.0)
-
-    run_items(work_items(count_s, order), BATCH_D, order, list_s, item)
+        return acc
+
+    def add(group, value):
+        total[group, 0] = total[group, 0] + value
+
+    number = work_items(count_v, items_v, items_s, ends, ends_v, ends_s, sem.at[1])
+    run_items(number, BATCH_D, items_s, list_s, item, add)
     scale = 1.0 / (4.0 * math.pi * safe * safe * safe)
-    for t in range(TILES):
-        both = folded(total[t], total[TILES + t])
-        sums[:, 128 * t : 128 * t + 128] = both * scale[:, 128 * t : 128 * t + 128]
+    sums[...] = row_sums(total, 0, 1, reduced) * scale
 
 
 def home_lanes():
@@ -334,9 +410,12 @@
 
 
 def force_kernel(
-    table, fresh, list_s, count_s, coord, home, pos, vel, mass, smooth, entropy, stored, count,
-    active, sums, density, order, rows, columns, total, natural,
+    table, fresh, list_v, count_v, coord, home, pos, vel, mass, smooth, entropy, stored, count,
+    active, sums, density, list_s, items_v, items_s, ends, ends_v, ends_s, rows, columns, total, reduced,
+    natural, sem,
 ):
+    list_copy = pltpu.make_async_copy(list_v, list_s, sem.at[0])
+    list_copy.start()
     is_cell = lax.broadcasted_iota(i32, (8, LANES), 1) < EXT
     live = lax.broadcasted_iota(i32, (8, LANES), 0).astype(f32) < table[LIVE : LIVE + 1, :]
     place = coord[...].astype(f32)
@@ -375,24 +454,23 @@
         start = pl.ds(pl.multiple_of(block * 8, 8), 8)
         cell = block * 8 + lax.broadcasted_iota(i32, (8, 256), 0)
         for c, value in enumerate((cell // 16, (cell // 4) % 4, cell % 4)):
-            store_columns(columns, c, block, natural[c, start, :] + value.astype(f32))
-            store_columns(columns, 3 + c, block, 20.0 * natural[3 + c, start, :])
+            store_columns(columns, c, block, 13, natural[c, start, :] + value.astype(f32))
+            store_columns(columns, 3 + c, block, 13, 20.0 * natural[3 + c, start, :])
         dens = natural[9, start, :]
         pressure, sound = state(natural[8, start, :], dens)
         for f, value in enumerate(features(natural[7, start, :], sound, dens, pressure)):
-            store_columns(columns, 6 + f, block, value)
-        store_columns(columns, 12, block, natural[6, start, :])
+            store_columns(columns, 6 + f, block, 13, value)
+        store_columns(columns, 12, block, 13, natural[6, start, :])
         return 0
 
     lax.fori_loop(0, CELLS // 8, fill, 0)
     columns[NONE] = jnp.ones((13, 8, 128), f32)
     columns[NONE, 12] = jnp.zeros((8, 128), f32)
     total[...] = jnp.zeros_like(total)
-    lane_index = lax.broadcasted_iota(i32, (8, 128), 1)
-
-    def item(tile, lane, cells):
-        at = lane_of(lane)
-        row = [jnp.take_along_axis(rows[f, tile], at, axis=1) for f in range(12)]
+    list_copy.wait()
+
+    def item(group, cells):
+        row = [rows[pl.ds(group * HELD + f, 8, stride=0), :] for f in range(12)]
         acc = [None] * 3
         for cell in cells:
             col = [columns[cell, f] for f in range(13)]
@@ -421,15 +499,16 @@
             for c in range(3):
                 term = weight * d[c]
                 acc[c] = term if acc[c] is None else acc[c] + term
-        mine = lane_index == lane
+        return acc
+
+    def add(group, values):
         for c in range(3):
-            summed = jnp.sum(acc[c], axis=1, keepdims=True)
-            total[c, tile] = total[c, tile] + jnp.where(mine, summed, 0.0)
-
-    run_items(work_items(count_s, order), BATCH_F, order, list_s, item)
+            total[group, c] = total[group, c] + values[c]
+
+    number = work_items(count_v, items_v, items_s, ends, ends_v, ends_s, sem.at[1])
+    run_items(number, BATCH_F, items_s, list_s, item, add)
     for c in range(3):
-        for t in range(TILES):
-            sums[8 * c : 8 * c + 8, 128 * t : 128 * t + 128] = folded(total[c, t], total[c, TILES + t])
+        sums[8 * c : 8 * c + 8, :] = row_sums(total, c, 3, reduced)
 
 
 def spread_kernel(pushed, home, active, out):
@@ -460,6 +539,30 @@
         scratch_shapes=list(scratch),
         compiler_params=PARAMS,
     )(*inputs)
+
+
+def item_scratch():
+    return [
+        pltpu.VMEM((ITEM_ROWS, 128), i32), pltpu.SMEM((ITEM_ROWS, 128), i32),
+        pltpu.VMEM((GROUPS, 128), f32), pltpu.VMEM((16, 128), f32), pltpu.SMEM((16, 128), f32),
+    ]
+
+
+def density_scratch():
+    return [
+        pltpu.VMEM((LIST_ROWS, 128), i32), pltpu.VMEM((16, 128), i32), pltpu.SMEM((LIST_ROWS, 128), i32),
+        *item_scratch(), pltpu.VMEM((GROUPS * HELD, 128), f32), pltpu.VMEM((CELLS + 1, 4, 8, 128), f32),
+        pltpu.VMEM((GROUPS, 1, 8, 128), f32), pltpu.VMEM((GROUPS, 128), f32),
+        pltpu.VMEM((4, CELLS, 256), f32), pltpu.SemaphoreType.DMA((2,)),
+    ]
+
+
+def force_scratch():
+    return [
+        pltpu.SMEM((LIST_ROWS, 128), i32), *item_scratch(), pltpu.VMEM((GROUPS * HELD, 128), f32), pltpu.VMEM((CELLS + 1, 13, 8, 128), f32),
+        pltpu.VMEM((GROUPS, 3, 8, 128), f32), pltpu.VMEM((GROUPS, 128), f32),
+        pltpu.VMEM((10, CELLS, 256), f32), pltpu.SemaphoreType.DMA((2,)),
+    ]
 
 
 def ring(axis, by):
@@ -553,16 +656,10 @@
         density_kernel,
         inputs,
         [
-            shape(ROWS, LANES), shape(28, GROUPS, dtype=i32), shape(1, GROUPS, dtype=i32),
+            shape(ROWS, LANES), shape(LIST_ROWS, 128, dtype=i32), shape(16, 128, dtype=i32),
             shape(ACT, LANES),
         ],
-        scratch=[
-            pltpu.VMEM((28, GROUPS), i32), pltpu.VMEM((1, GROUPS), i32),
-            pltpu.SMEM((28, GROUPS), i32), pltpu.SMEM((1, GROUPS), i32),
-            pltpu.SMEM((GROUPS + 128,), i32), pltpu.VMEM((4, 2 * TILES, 8, 128), f32),
-            pltpu.VMEM((CELLS + 1, 4, 8, 128), f32), pltpu.VMEM((2 * TILES, 8, 128), f32),
-            pltpu.VMEM((4, CELLS, 256), f32), pltpu.SemaphoreType.DMA((2,)),
-        ],
+        scratch=density_scratch(),
     )
     fresh = shared_sums(sums, coord)
     inputs = (
@@ -573,12 +670,8 @@
         force_kernel,
         inputs,
         [shape(24, LANES), shape(BX, BY, BZ, 256)],
-        in_specs=[VMEM_SPEC, VMEM_SPEC, SMEM_SPEC, SMEM_SPEC] + [VMEM_SPEC] * 10,
-        scratch=[
-            pltpu.SMEM((GROUPS + 128,), i32), pltpu.VMEM((12, 2 * TILES, 8, 128), f32),
-            pltpu.VMEM((CELLS + 1, 13, 8, 128), f32), pltpu.VMEM((3, 2 * TILES, 8, 128), f32),
-            pltpu.VMEM((10, CELLS, 256), f32),
-        ],
+
+        scratch=force_scratch(),
     )
     pushed = returned_sums(sums, coord)
     acceleration = call(spread_kernel, (pushed, home, active), shape(3, BX, BY, BZ, 256))

time: 437 us -> 234 us (0.54); the launches traced: 441 us -> 232 us
  Pallas kernels: 366 us -> 161 us
    pallas_call x4, Pallas kernels: 366 us -> 161 us  [call(): pl.pallas_call(kernel, out_shape=outputs, in_specs=in_specs or [VMEM_SPEC...]
where the time goes in v1:
time: 234 us; the launch traced here: 232 us
  Pallas kernels  161 us (69%)
  waiting for transfers between devices  36.1 us (15%)
  starting transfers between devices  18.1 us (8%)
  local copies, waits for them, and re-layouts  11.3 us (5%)
  other arithmetic  4.33 us (2%)
    pallas_call x4, Pallas kernels, call(): pl.pallas_call(kernel, out_shape=outputs, in_specs=in_specs or [VMEM_SPEC...  161 us
    ppermute x2, waiting for transfers between devices, returned_sums(): other = lax.ppermute(sums, axis, ring(axis, 1))  8.22 us
    ppermute x2, waiting for transfers between devices, shared_sums(): other = lax.ppermute(sums, axis, ring(axis, 1))  7.93 us
    ppermute x1, waiting for transfers between devices, returned_sums(): before = lax.ppermute(sums[:, top + plane:EXT], 'gx', ring('gx', 1))  6.27 us
    ppermute x1, waiting for transfers between devices, first_exchange(): before = lax.ppermute(high, 'gx', ring('gx', 1))  5.28 us
    ppermute x1, starting transfers between devices, shared_sums(): after = lax.ppermute(sums[:, :2 * plane], 'gx', ring('gx', -1))  5.06 us
    ppermute x1, waiting for transfers between devices, first_exchange(): edge_in = lax.ppermute(edge, across, [(0, 3), (1, 2), (2, 1), (3, 0)])  4.91 us
  transfers between devices with their start and end apart: 13, of which 10 were waited for; matrix products, arithmetic and copies ran while one was open for 1% of the time, Pallas kernels for 0%

profile of v1, /device:TPU:0, one launch (start us, length us, event | category | flops | bytes accessed | tf_op | source)
XLA Modules:
  0.0 232.1 jit_solution(413614634704075844)
XLA Ops:
  3.3 3.9 %shard_map.140 = (f32[112,256]{1,0:T(8,128)}, f32[112,384]{1,0:T(8,128)}) custom-call(f32[3,16,4,4,256]{4,3,2,1,0:T(4,128)} %pos.5, f32[3,16,4,4,256]{4,3,2,1,0:T(4,128)} %vel.3, f32[16,4,4,256]{3,2,1,0:T(4,128)} %mass.5, f32[16,4,4,256]{3,2,1,0:T(4,128)} %smooth.3, f32[16,4,4,256]{3,2,1,0:T(4,128)} %entropy.3, f32[16,4,4,256]{3,2,1,0:T(4,128)} %stored.3, ...), custom_call_target="tpu_custom_call" | custom-call | tf_op jit(solution)/shard_map/pallas_call | solution.py:534
  7.2 0.9 fusion.4
  8.1 1.7 collective-permute-start.1
  9.7 2.7 %collective-permute-start = (f32[112,128]{1,0:T(8,128)S(1)}, f32[112,128]{1,0:T(8,128)S(1)}, u32[]{:S(2)}, u32[]{:S(2)}) collective-permute-start(f32[112,128]{1,0:T(8,128)S(1)} %get-tuple-element.19), channel_id=1, source_target_pairs={{0,2},{1,3},{2,0},{3,1},{4,6},{5,7},{6,4},{7,5},{8,10},{9,11},{10,... | collective-permute-start | bytes 172040 | tf_op jit(solution)/shard_map/ppermute | solution.py:576
  12.5 0.8 slice.124
  13.8 4.9 %collective-permute-done.2 = f32[112,64]{1,0:T(8,128)S(1)} collective-permute-done((f32[112,64]{1,0:T(8,128)S(1)}, f32[112,64]{1,0:T(8,128)S(1)}, u32[]{:S(2)}, u32[]{:S(2)}) %collective-permute-start.2) | collective-permute-done | bytes 28704 | tf_op jit(solution)/shard_map/ppermute | solution.py:578
  19.0 4.3 %collective-permute-start.4 = (f32[112,36]{1,0:T(8,128)S(1)}, f32[112,36]{1,0:T(8,128)S(1)}, u32[]{:S(2)}, u32[]{:S(2)}) collective-permute-start(f32[112,36]{1,0:T(8,128)S(1)} %pad_maximum_fusion.1), channel_id=1, source_target_pairs={{0,124},{4,0},{8,4},{12,8},{16,12},{20,16},{24,20},{28,24},{32,28}... | collective-permute-start | bytes 48392 | tf_op jit(solution)/shard_map/ppermute | solution.py:582
  23.5 1.6 collective-permute-done.4
  25.2 5.3 %collective-permute-done.3 = f32[112,36]{1,0:T(8,128)S(1)} collective-permute-done((f32[112,36]{1,0:T(8,128)S(1)}, f32[112,36]{1,0:T(8,128)S(1)}, u32[]{:S(2)}, u32[]{:S(2)}) %collective-permute-start.3) | collective-permute-done | bytes 16160 | tf_op jit(solution)/shard_map/ppermute | solution.py:581
  30.4 0.8 concatenate.45.parts
  31.3 52.1 %shard_map.141 = (f32[112,768]{1,0:T(8,128)}, s32[112,128]{1,0:T(8,128)}, s32[16,128]{1,0:T(8,128)}, f32[8,768]{1,0:T(8,128)}) custom-call(f32[112,768]{1,0:T(8,128)} %concatenate.45.parts, s32[8,768]{1,0:T(8,128)} %constant.7.clone.coord, s32[8,768]{1,0:T(8,128)} %constant.8.clone.source, f32[3,16,4,4,256]{4,3,2,1,0:T(4,128)} %pos.5, ...), custom_call_target="tpu_custom_call" | custom-call | tf_op jit(solution)/shard_map/pallas_call | solution.py:534
  83.4 0.8 fusion.17
  84.2 5.1 %collective-permute-start.6 = (f32[8,72]{1,0:T(8,128)S(1)}, f32[8,72]{1,0:T(8,128)S(1)}, u32[]{:S(2)}, u32[]{:S(2)}) collective-permute-start(f32[8,72]{1,0:T(8,128)S(1)} %get-tuple-element.49), channel_id=1, source_target_pairs={{0,124},{4,0},{8,4},{12,8},{16,12},{20,16},{24,20},{28,24},{32,28}... | collective-permute-start | bytes 6920 | tf_op jit(solution)/shard_map/ppermute | solution.py:597
  90.8 5.3 %collective-permute-done.7 = f32[8,768]{1,0:T(8,128)S(1)} collective-permute-done((f32[8,768]{1,0:T(8,128)S(1)}, f32[8,768]{1,0:T(8,128)S(1)}, u32[]{:S(2)}, u32[]{:S(2)}) %collective-permute-start.7) | collective-permute-done | bytes 24608 | tf_op jit(solution)/shard_map/ppermute | solution.py:603
  98.5 2.6 %collective-permute-done.8 = f32[8,768]{1,0:T(8,128)S(1)} collective-permute-done((f32[8,768]{1,0:T(8,128)S(1)}, f32[8,768]{1,0:T(8,128)S(1)}, u32[]{:S(2)}, u32[]{:S(2)}) %collective-permute-start.8) | collective-permute-done | bytes 24608 | tf_op jit(solution)/shard_map/ppermute | solution.py:603
  102.6 102.0 %shard_map.142 = (f32[24,768]{1,0:T(8,128)}, f32[16,4,4,256]{3,2,1,0:T(4,128)}) custom-call(f32[112,768]{1,0:T(8,128)} %get-tuple-element.12.table, f32[8,768]{1,0:T(8,128)} %fusion.3.fresh, s32[112,128]{1,0:T(8,128)} %get-tuple-element.14.list_v, s32[16,128]{1,0:T(8,128)} %get-tuple-element.15.count_v, s32[8,768]{1,0:T(8,128)} %constant.7.clone.coord, ...), custom_call_target="tpu_custom_call" | custom-call | tf_op jit(solution)/shard_map/pallas_call | solution.py:534
  205.4 1.1 collective-permute-start.10
  206.5 1.4 collective-permute-done.10
  207.9 0.9 slice_add_fusion
  209.0 6.3 %collective-permute-done.9 = f32[24,36]{1,0:T(8,128)S(1)} collective-permute-done((f32[24,36]{1,0:T(8,128)S(1)}, f32[24,36]{1,0:T(8,128)S(1)}, u32[]{:S(2)}, u32[]{:S(2)}) %collective-permute-start.9) | collective-permute-done | bytes 3488 | tf_op jit(solution)/shard_map/ppermute | solution.py:614
  215.6 5.9 %collective-permute-done.11 = f32[24,768]{1,0:T(8,128)S(1)} collective-permute-done((f32[24,768]{1,0:T(8,128)S(1)}, f32[24,768]{1,0:T(8,128)S(1)}, u32[]{:S(2)}, u32[]{:S(2)}) %collective-permute-start.11) | collective-permute-done | bytes 73760 | tf_op jit(solution)/shard_map/ppermute | solution.py:627
  222.4 2.4 %collective-permute-start.12 = (f32[24,768]{1,0:T(8,128)S(1)}, f32[24,768]{1,0:T(8,128)S(1)}, u32[]{:S(2)}, u32[]{:S(2)}) collective-permute-start(f32[24,768]{1,0:T(8,128)S(1)} %fusion), channel_id=1, source_target_pairs={{0,1},{1,0},{2,3},{3,2},{4,5},{5,4},{6,7},{7,6},{8,9},{9,8},{10,11... | collective-permute-start | bytes 221192 | tf_op jit(solution)/shard_map/ppermute | solution.py:627
  224.8 2.3 %collective-permute-done.12 = f32[24,768]{1,0:T(8,128)S(1)} collective-permute-done((f32[24,768]{1,0:T(8,128)S(1)}, f32[24,768]{1,0:T(8,128)S(1)}, u32[]{:S(2)}, u32[]{:S(2)}) %collective-permute-start.12) | collective-permute-done | bytes 73760 | tf_op jit(solution)/shard_map/ppermute | solution.py:627
  228.7 3.4 %shard_map.143 = f32[3,16,4,4,256]{4,3,2,1,0:T(4,128)} custom-call(f32[24,768]{1,0:T(8,128)} %fusion.1.pushed, s32[8,256]{1,0:T(8,128)} %constant.22.clone.home, s32[256,1]{1,0:T(8,128)} %reshape.29.active), custom_call_target="tpu_custom_call" | custom-call | tf_op jit(solution)/shard_map/pallas_call | solution.py:534
  (79 shorter events, 12.8 us)
Async XLA Ops:
  0.6 0.9 copy-start.5
  1.3 1.1 copy-start.2
  8.1 5.6 %copy-start = (f32[112,256]{1,0:T(8,128)S(1)}, f32[112,256]{1,0:T(8,128)}, u32[]{:S(2)}) copy-start(f32[112,256]{1,0:T(8,128)} %get-tuple-element.10) | copy-start | bytes 344068
  8.1 10.8 %collective-permute-start.1 = (f32[112,128]{1,0:T(8,128)S(1)}, f32[112,128]{1,0:T(8,128)S(1)}, u32[]{:S(2)}, u32[]{:S(2)}) collective-permute-start(f32[112,128]{1,0:T(8,128)S(1)} %get-tuple-element.18), channel_id=1, source_target_pairs={{0,1},{1,0},{2,3},{3,2},{4,5},{5,4},{6,7},{7,6},{8,9},{9,8},{10,11... | collective-permute-start | bytes 172040 | tf_op jit(solution)/shard_map/ppermute | solution.py:577
  9.7 9.0 %collective-permute-start = (f32[112,128]{1,0:T(8,128)S(1)}, f32[112,128]{1,0:T(8,128)S(1)}, u32[]{:S(2)}, u32[]{:S(2)}) collective-permute-start(f32[112,128]{1,0:T(8,128)S(1)} %get-tuple-element.19), channel_id=1, source_target_pairs={{0,2},{1,3},{2,0},{3,1},{4,6},{5,7},{6,4},{7,5},{8,10},{9,11},{10,... | collective-permute-start | bytes 172040 | tf_op jit(solution)/shard_map/ppermute | solution.py:576
  13.3 5.4 %collective-permute-start.2 = (f32[112,64]{1,0:T(8,128)S(1)}, f32[112,64]{1,0:T(8,128)S(1)}, u32[]{:S(2)}, u32[]{:S(2)}) collective-permute-start(f32[112,64]{1,0:T(8,128)S(1)} %slice.124), channel_id=1, source_target_pairs={{0,3},{1,2},{2,1},{3,0},{4,7},{5,6},{6,5},{7,4},{8,11},{9,10},{10,... | collective-permute-start | bytes 86024 | tf_op jit(solution)/shard_map/ppermute | solution.py:578
  19.0 6.1 %collective-permute-start.4 = (f32[112,36]{1,0:T(8,128)S(1)}, f32[112,36]{1,0:T(8,128)S(1)}, u32[]{:S(2)}, u32[]{:S(2)}) collective-permute-start(f32[112,36]{1,0:T(8,128)S(1)} %pad_maximum_fusion.1), channel_id=1, source_target_pairs={{0,124},{4,0},{8,4},{12,8},{16,12},{20,16},{24,20},{28,24},{32,28}... | collective-permute-start | bytes 48392 | tf_op jit(solution)/shard_map/ppermute | solution.py:582
  23.4 7.0 %collective-permute-start.3 = (f32[112,36]{1,0:T(8,128)S(1)}, f32[112,36]{1,0:T(8,128)S(1)}, u32[]{:S(2)}, u32[]{:S(2)}) collective-permute-start(f32[112,36]{1,0:T(8,128)S(1)} %pad_maximum_fusion), channel_id=1, source_target_pairs={{0,4},{4,8},{8,12},{12,16},{16,20},{20,24},{24,28},{28,32},{32,36}... | collective-permute-start | bytes 48392 | tf_op jit(solution)/shard_map/ppermute | solution.py:581
  83.4 6.7 %copy-start.3 = (f32[8,768]{1,0:T(8,128)S(1)}, f32[8,768]{1,0:T(8,128)}, u32[]{:S(2)}) copy-start(f32[8,768]{1,0:T(8,128)} %get-tuple-element.13) | copy-start | bytes 73732
  84.2 6.4 %collective-permute-start.5 = (f32[8,72]{1,0:T(8,128)S(1)}, f32[8,72]{1,0:T(8,128)S(1)}, u32[]{:S(2)}, u32[]{:S(2)}) collective-permute-start(f32[8,72]{1,0:T(8,128)S(1)} %get-tuple-element.48), channel_id=1, source_target_pairs={{0,4},{4,8},{8,12},{12,16},{16,20},{20,24},{24,28},{28,32},{32,36}... | collective-permute-start | bytes 6920 | tf_op jit(solution)/shard_map/ppermute | solution.py:596
  84.2 6.4 %collective-permute-start.6 = (f32[8,72]{1,0:T(8,128)S(1)}, f32[8,72]{1,0:T(8,128)S(1)}, u32[]{:S(2)}, u32[]{:S(2)}) collective-permute-start(f32[8,72]{1,0:T(8,128)S(1)} %get-tuple-element.49), channel_id=1, source_target_pairs={{0,124},{4,0},{8,4},{12,8},{16,12},{20,16},{24,20},{28,24},{32,28}... | collective-permute-start | bytes 6920 | tf_op jit(solution)/shard_map/ppermute | solution.py:597
  90.8 5.4 %collective-permute-start.7 = (f32[8,768]{1,0:T(8,128)S(1)}, f32[8,768]{1,0:T(8,128)S(1)}, u32[]{:S(2)}, u32[]{:S(2)}) collective-permute-start(f32[8,768]{1,0:T(8,128)S(1)} %pad_maximum_fusion.2), channel_id=1, source_target_pairs={{0,2},{2,0},{1,3},{3,1},{4,6},{6,4},{5,7},{7,5},{8,10},{10,8},{9,1... | collective-permute-start | bytes 73736 | tf_op jit(solution)/shard_map/ppermute | solution.py:603
  96.3 0.7 copy-start.12
  96.9 0.7 copy-start.4
  97.0 4.1 %collective-permute-start.8 = (f32[8,768]{1,0:T(8,128)S(1)}, f32[8,768]{1,0:T(8,128)S(1)}, u32[]{:S(2)}, u32[]{:S(2)}) collective-permute-start(f32[8,768]{1,0:T(8,128)S(1)} %fusion.2), channel_id=1, source_target_pairs={{0,1},{1,0},{2,3},{3,2},{4,5},{5,4},{6,7},{7,6},{8,9},{9,8},{10,11... | collective-permute-start | bytes 73736 | tf_op jit(solution)/shard_map/ppermute | solution.py:603
  101.3 0.7 copy-start.10
  204.7 4.2 %copy-start.1 = (f32[24,768]{1,0:T(8,128)S(1)}, f32[24,768]{1,0:T(8,128)}, u32[]{:S(2)}) copy-start(f32[24,768]{1,0:T(8,128)} %get-tuple-element.17) | copy-start | bytes 221188
  205.4 2.5 %collective-permute-start.10 = (f32[24,36]{1,0:T(8,128)S(1)}, f32[24,36]{1,0:T(8,128)S(1)}, u32[]{:S(2)}, u32[]{:S(2)}) collective-permute-start(f32[24,36]{1,0:T(8,128)S(1)} %slice.147), channel_id=1, source_target_pairs={{0,124},{4,0},{8,4},{12,8},{16,12},{20,16},{24,20},{28,24},{32,28}... | collective-permute-start | bytes 10376 | tf_op jit(solution)/shard_map/ppermute | solution.py:615
  208.8 6.4 %collective-permute-start.9 = (f32[24,36]{1,0:T(8,128)S(1)}, f32[24,36]{1,0:T(8,128)S(1)}, u32[]{:S(2)}, u32[]{:S(2)}) collective-permute-start(f32[24,36]{1,0:T(8,128)S(1)} %get-tuple-element.31), channel_id=1, source_target_pairs={{0,4},{4,8},{8,12},{12,16},{16,20},{20,24},{24,28},{28,32},{32,36}... | collective-permute-start | bytes 10376 | tf_op jit(solution)/shard_map/ppermute | solution.py:614
  215.5 6.0 %collective-permute-start.11 = (f32[24,768]{1,0:T(8,128)S(1)}, f32[24,768]{1,0:T(8,128)S(1)}, u32[]{:S(2)}, u32[]{:S(2)}) collective-permute-start(f32[24,768]{1,0:T(8,128)S(1)} %concatenate.51), channel_id=1, source_target_pairs={{0,2},{2,0},{1,3},{3,1},{4,6},{6,4},{5,7},{7,5},{8,10},{10,8},{9,1... | collective-permute-start | bytes 221192 | tf_op jit(solution)/shard_map/ppermute | solution.py:627
  221.5 0.7 copy-start.9
  221.6 0.7 copy-start.8
  222.4 4.8 %collective-permute-start.12 = (f32[24,768]{1,0:T(8,128)S(1)}, f32[24,768]{1,0:T(8,128)S(1)}, u32[]{:S(2)}, u32[]{:S(2)}) collective-permute-start(f32[24,768]{1,0:T(8,128)S(1)} %fusion), channel_id=1, source_target_pairs={{0,1},{1,0},{2,3},{3,2},{4,5},{5,4},{6,7},{7,6},{8,9},{9,8},{10,11... | collective-permute-start | bytes 221192 | tf_op jit(solution)/shard_map/ppermute | solution.py:627
  227.3 0.7 copy-start.6
  (3 other events, 2.0 us)

commit v2 on v1

--- a/solution.py
+++ b/solution.py
@@ -24,9 +24,9 @@
 WORDS = 9
 ITEM_ROWS = 96
 LIST_ROWS = 112
-HELD = 16
+HELD = 13
 BATCH_D = 8
-BATCH_F = 4
+BATCH_F = 8
 NONE = CELLS
 ADIABATIC = 5.0 / 3.0
 HIGHEST = lax.Precision.HIGHEST
@@ -317,16 +317,16 @@
 
 def row_sums(tiles, part_index, count, reduced):
     def block(i, _):
-        for u in range(4):
+        for u in range(16):
             value = None
             for s in range(8):
-                at = ((i * 32 + u * 8) * count + part_index) * 8 + s
+                at = ((i * 128 + u * 8) * count + part_index) * 8 + s
                 part = tiles.reshape(GROUPS * count * 8, 128)[pl.ds(at, 8, stride=8 * count), :]
                 value = part if value is None else value + part
-            reduced[pl.ds(pl.multiple_of(i * 32 + u * 8, 8), 8), :] = value
+            reduced[pl.ds(pl.multiple_of(i * 128 + u * 8, 8), 8), :] = value
         return 0
 
-    lax.fori_loop(0, GROUPS // 32, block, 0)
+    lax.fori_loop(0, GROUPS // 128, block, 0)
     row = lax.broadcasted_iota(i32, (8, 128), 0)
     segment = lax.broadcasted_iota(i32, (8, 128), 1) // 32
     out = None
@@ -362,15 +362,19 @@
         natural[c] = pos[c].reshape(CELLS, 256)
     natural[3] = live_mass(mass[...].reshape(CELLS, 256), count[...])
 
-    def fill(block, _):
+    def fill_block(block):
         start = pl.ds(pl.multiple_of(block * 8, 8), 8)
         cell = block * 8 + lax.broadcasted_iota(i32, (8, 256), 0)
         for c, value in enumerate((cell // 16, (cell // 4) % 4, cell % 4)):
             store_columns(columns, c, block, 4, natural[c, start, :] + value.astype(f32))
         store_columns(columns, 3, block, 4, natural[3, start, :])
+
+    def fill(step, _):
+        for u in range(4):
+            fill_block(step * 4 + u)
         return 0
 
-    lax.fori_loop(0, CELLS // 8, fill, 0)
+    lax.fori_loop(0, CELLS // 32, fill, 0)
     columns[NONE] = jnp.zeros((4, 8, 128), f32)
     total[...] = jnp.zeros_like(total)
     list_copy.wait()
@@ -398,6 +402,26 @@
     sums[...] = row_sums(total, 0, 1, reduced) * scale
 
 
+def joined(sums, along_y, along_z, along_both, coord, shared):
+    def matched(values, axis):
+        step, extent = ((EZ, BY), (1, BZ))[axis - 1]
+        position = coord[axis : axis + 1, :]
+        low = position == 0
+        high = position == extent - 1
+        if shared:
+            low = low | (position == -1)
+            high = high | (position == extent)
+        by = extent * step
+        ahead = pltpu.roll(values, LANES - by, 1)
+        behind = pltpu.roll(values, by, 1)
+        return jnp.where(low, ahead, jnp.where(high, behind, 0.0))
+
+    return (
+        sums[...] + matched(along_y[...], 1) + matched(along_z[...], 2)
+        + matched(matched(along_both[...], 1), 2)
+    )
+
+
 def home_lanes():
     cell = np.arange(CELLS)
     lane = ((cell // 16 + 1) * EY + (cell // 4) % 4 + 1) * EZ + cell % 4 + 1
@@ -410,7 +434,7 @@
 
 
 def force_kernel(
-    table, fresh, list_v, count_v, coord, home, pos, vel, mass, smooth, entropy, stored, count,
+    table, fresh, fresh_y, fresh_z, fresh_yz, list_v, count_v, coord, home, pos, vel, mass, smooth, entropy, stored, count,
     active, sums, density, list_s, items_v, items_s, ends, ends_v, ends_s, rows, columns, total, reduced,
     natural, sem,
 ):
@@ -423,7 +447,8 @@
     def field(f):
         return table[8 * f : 8 * f + 8, :]
 
-    rho = jnp.where(is_cell, jnp.where(live, fresh[...], field(9)), 1.0)
+    now = joined(fresh, fresh_y, fresh_z, fresh_yz, coord, True)
+    rho = jnp.where(is_cell, jnp.where(live, now, field(9)), 1.0)
     row_h = jnp.where(is_cell, field(4), 1.0)
     row_p, row_s = state(field(8), rho)
 
@@ -450,7 +475,7 @@
     natural[8] = entropy[...].reshape(CELLS, 256)
     natural[9] = new
 
-    def fill(block, _):
+    def fill_block(block):
         start = pl.ds(pl.multiple_of(block * 8, 8), 8)
         cell = block * 8 + lax.broadcasted_iota(i32, (8, 256), 0)
         for c, value in enumerate((cell // 16, (cell // 4) % 4, cell % 4)):
@@ -461,9 +486,13 @@
         for f, value in enumerate(features(natural[7, start, :], sound, dens, pressure)):
             store_columns(columns, 6 + f, block, 13, value)
         store_columns(columns, 12, block, 13, natural[6, start, :])
+
+    def fill(step, _):
+        for u in range(2):
+            fill_block(step * 2 + u)
         return 0
 
-    lax.fori_loop(0, CELLS // 8, fill, 0)
+    lax.fori_loop(0, CELLS // 16, fill, 0)
     columns[NONE] = jnp.ones((13, 8, 128), f32)
     columns[NONE, 12] = jnp.zeros((8, 128), f32)
     total[...] = jnp.zeros_like(total)
@@ -511,8 +540,9 @@
         sums[8 * c : 8 * c + 8, :] = row_sums(total, c, 3, reduced)
 
 
-def spread_kernel(pushed, home, active, out):
-    mine = picked(pushed[...], home[0:1, :])
+def spread_kernel(pushed, pushed_y, pushed_z, pushed_yz, coord, home, active, out):
+    whole = joined(pushed, pushed_y, pushed_z, pushed_yz, coord, False)
+    mine = picked(whole, home[0:1, :])
     slot = lax.broadcasted_iota(i32, (CELLS, 128), 1)
     for c in range(3):
         rows = lanes_to_cells(mine[8 * c : 8 * c + 8, :])
@@ -572,10 +602,10 @@
 
 def first_exchange(table, faces):
     y_part, z_part, edge = faces[:, :128], faces[:, 128:256], faces[:, 256:320]
-    across = ("gy", "gz")
-    y_in = lax.ppermute(y_part, across, [(0, 2), (1, 3), (2, 0), (3, 1)])
-    z_in = lax.ppermute(z_part, across, [(0, 1), (1, 0), (2, 3), (3, 2)])
-    edge_in = lax.ppermute(edge, across, [(0, 3), (1, 2), (2, 1), (3, 0)])
+    y_in, z_in, edge_in = (
+        lax.ppermute(part, ("gy", "gz"), pairs)
+        for part, pairs in zip((y_part, z_part, edge), ACROSS)
+    )
     low = jnp.concatenate([table[:, :16], y_in[:, :8], z_in[:, :8], edge_in[:, :4]], 1)
     high = jnp.concatenate([table[:, 240:], y_in[:, 120:], z_in[:, 120:], edge_in[:, 60:]], 1)
     before = lax.ppermute(high, "gx", ring("gx", 1))
@@ -584,36 +614,34 @@
     return jnp.concatenate([table, y_in, z_in, edge_in, before, after, unused], 1)
 
 
-def turned(values, by):
-    return jnp.concatenate([values[:, -by:], values[:, :-by]], 1) if by > 0 else jnp.concatenate(
-        [values[:, -by:], values[:, :-by]], 1
-    )
-
-
-def shared_sums(sums, coord):
+ACROSS = (
+    [(0, 2), (1, 3), (2, 0), (3, 1)],
+    [(0, 1), (1, 0), (2, 3), (3, 2)],
+    [(0, 3), (1, 2), (2, 1), (3, 0)],
+)
+
+
+def sent_across(sums):
+    return [lax.ppermute(sums, ("gy", "gz"), pairs) for pairs in ACROSS]
+
+
+def shared_sums(sums):
     plane = EY * EZ
     top = BX * plane
     before = lax.ppermute(sums[:, top : top + 2 * plane], "gx", ring("gx", 1))
     after = lax.ppermute(sums[:, : 2 * plane], "gx", ring("gx", -1))
     middle = sums[:, 2 * plane : top]
-    sums = jnp.concatenate(
+    return jnp.concatenate(
         [sums[:, : 2 * plane] + before, middle, sums[:, top:EXT] + after, sums[:, EXT:]], 1
     )
-    for axis, step, position, extent in (("gy", EZ, coord[1:2], BY), ("gz", 1, coord[2:3], BZ)):
-        other = lax.ppermute(sums, axis, ring(axis, 1))
-        shift = extent * step
-        low = (position == -1) | (position == 0)
-        high = (position == extent - 1) | (position == extent)
-        sums = sums + jnp.where(low, turned(other, -shift), jnp.where(high, turned(other, shift), 0.0))
-    return sums
-
-
-def returned_sums(sums, coord):
+
+
+def returned_sums(sums):
     plane = EY * EZ
     top = BX * plane
     before = lax.ppermute(sums[:, top + plane : EXT], "gx", ring("gx", 1))
     after = lax.ppermute(sums[:, :plane], "gx", ring("gx", -1))
-    sums = jnp.concatenate(
+    return jnp.concatenate(
         [
             sums[:, :plane],
             sums[:, plane : 2 * plane] + before,
@@ -623,15 +651,6 @@
         ],
         1,
     )
-    for axis, step, position, extent in (("gy", EZ, coord[1:2], BY), ("gz", 1, coord[2:3], BZ)):
-        other = lax.ppermute(sums, axis, ring(axis, 1))
-        shift = extent * step
-        sums = sums + jnp.where(
-            position == 0,
-            turned(other, -shift),
-            jnp.where(position == extent - 1, turned(other, shift), 0.0),
-        )
-    return sums
 
 
 def shards(pos, vel, mass, smooth, entropy, stored, particle_count, active_count, pair_side):
@@ -661,9 +680,9 @@
         ],
         scratch=density_scratch(),
     )
-    fresh = shared_sums(sums, coord)
+    fresh = shared_sums(sums)
     inputs = (
-        table, fresh, list_f, count_f, coord, home, pos, vel, mass, smooth, entropy, stored,
+        table, fresh, *sent_across(fresh), list_f, count_f, coord, home, pos, vel, mass, smooth, entropy, stored,
         count, active,
     )
     sums, density = call(
@@ -673,8 +692,9 @@
 
         scratch=force_scratch(),
     )
-    pushed = returned_sums(sums, coord)
-    acceleration = call(spread_kernel, (pushed, home, active), shape(3, BX, BY, BZ, 256))
+    pushed = returned_sums(sums)
+    inputs = (pushed, *sent_across(pushed), coord, home, active)
+    acceleration = call(spread_kernel, inputs, shape(3, BX, BY, BZ, 256))
     return density, acceleration
 
 

time: 234 us -> 219 us (0.936)
  starting transfers between devices: 18.1 us -> 27.3 us
  waiting for transfers between devices: 36.1 us -> 27 us
  Pallas kernels: 161 us -> 152 us
  local copies, waits for them, and re-layouts: 11.3 us -> 8.9 us
    pallas_call x4, Pallas kernels: 161 us -> 152 us  [call(): pl.pallas_call(kernel, out_shape=outputs, in_specs=in_specs or [VMEM_SPEC...]
    ppermute x7 -> x9, waiting for transfers between devices: 21.1 us -> 11.9 us  [the longest x6 6.96 us: sent_across(): return [lax.ppermute(sums, ('gy', 'gz'), pairs) for pairs in ACROSS]]
    ppermute x7 -> x9, starting transfers between devices: 7.58 us -> 15.7 us  [the longest x6 10.9 us: sent_across(): return [lax.ppermute(sums, ('gy', 'gz'), pairs) for pairs in ACROSS]]
  transfers between devices with their start and end apart: 13 -> 15, of which waited for: 10 -> 9; matrix products, arithmetic and copies ran while one was open for 1% -> 1% of each run, Pallas kernels for 0% -> 0%
where the time goes in v2:
time: 219 us; the launch traced here: 218 us
  Pallas kernels  152 us (69%)
  starting transfers between devices  27.3 us (12%)
  waiting for transfers between devices  27 us (12%)
  local copies, waits for them, and re-layouts  8.9 us (4%)
  other arithmetic  2.75 us (1%)
    pallas_call x4, Pallas kernels, call(): pl.pallas_call(kernel, out_shape=outputs, in_specs=in_specs or [VMEM_SPEC...  152 us
    ppermute x6, starting transfers between devices, sent_across(): return [lax.ppermute(sums, ('gy', 'gz'), pairs) for pairs in ACROSS]  10.9 us
    ppermute x6, waiting for transfers between devices, sent_across(): return [lax.ppermute(sums, ('gy', 'gz'), pairs) for pairs in ACROSS]  6.96 us
    ppermute x1, waiting for transfers between devices, returned_sums(): before = lax.ppermute(sums[:, top + plane:EXT], 'gx', ring('gx', 1))  6.27 us
    ppermute x1, waiting for transfers between devices, first_exchange(): before = lax.ppermute(high, 'gx', ring('gx', 1))  5.28 us
    ppermute x1, starting transfers between devices, shared_sums(): after = lax.ppermute(sums[:, :2 * plane], 'gx', ring('gx', -1))  5.06 us
    ppermute x3, waiting for transfers between devices, first_exchange(): lax.ppermute(part, ('gy', 'gz'), pairs)  4.92 us
    ppermute x3, starting transfers between devices, first_exchange(): lax.ppermute(part, ('gy', 'gz'), pairs)  4.78 us
  transfers between devices with their start and end apart: 15, of which 9 were waited for; matrix products, arithmetic and copies ran while one was open for 1% of the time, Pallas kernels for 0%

profile of v2, /device:TPU:0, one launch (start us, length us, event | category | flops | bytes accessed | tf_op | source)
XLA Modules:
  0.0 218.5 jit_solution(18059657417627378045)
XLA Ops:
  3.3 3.9 %shard_map.140 = (f32[112,256]{1,0:T(8,128)}, f32[112,384]{1,0:T(8,128)}) custom-call(f32[3,16,4,4,256]{4,3,2,1,0:T(4,128)} %pos.5, f32[3,16,4,4,256]{4,3,2,1,0:T(4,128)} %vel.3, f32[16,4,4,256]{3,2,1,0:T(4,128)} %mass.5, f32[16,4,4,256]{3,2,1,0:T(4,128)} %smooth.3, f32[16,4,4,256]{3,2,1,0:T(4,128)} %entropy.3, f32[16,4,4,256]{3,2,1,0:T(4,128)} %stored.3, ...), custom_call_target="tpu_custom_call" | custom-call | tf_op jit(solution)/shard_map/pallas_call | solution.py:564
  7.2 0.9 fusion
  8.1 1.7 collective-permute-start.1
  9.7 2.7 %collective-permute-start = (f32[112,128]{1,0:T(8,128)S(1)}, f32[112,128]{1,0:T(8,128)S(1)}, u32[]{:S(2)}, u32[]{:S(2)}) collective-permute-start(f32[112,128]{1,0:T(8,128)S(1)} %get-tuple-element.19), channel_id=1, source_target_pairs={{0,2},{1,3},{2,0},{3,1},{4,6},{5,7},{6,4},{7,5},{8,10},{9,11},{10,... | collective-permute-start | bytes 172040 | tf_op jit(solution)/shard_map/ppermute | solution.py:606
  13.8 4.9 %collective-permute-done.2 = f32[112,64]{1,0:T(8,128)S(1)} collective-permute-done((f32[112,64]{1,0:T(8,128)S(1)}, f32[112,64]{1,0:T(8,128)S(1)}, u32[]{:S(2)}, u32[]{:S(2)}) %collective-permute-start.2) | collective-permute-done | bytes 28704 | tf_op jit(solution)/shard_map/ppermute | solution.py:606
  19.0 4.3 %collective-permute-start.4 = (f32[112,36]{1,0:T(8,128)S(1)}, f32[112,36]{1,0:T(8,128)S(1)}, u32[]{:S(2)}, u32[]{:S(2)}) collective-permute-start(f32[112,36]{1,0:T(8,128)S(1)} %pad_maximum_fusion.1), channel_id=1, source_target_pairs={{0,124},{4,0},{8,4},{12,8},{16,12},{20,16},{24,20},{28,24},{32,28}... | collective-permute-start | bytes 48392 | tf_op jit(solution)/shard_map/ppermute | solution.py:612
  23.5 1.6 collective-permute-done.4
  25.2 5.3 %collective-permute-done.3 = f32[112,36]{1,0:T(8,128)S(1)} collective-permute-done((f32[112,36]{1,0:T(8,128)S(1)}, f32[112,36]{1,0:T(8,128)S(1)}, u32[]{:S(2)}, u32[]{:S(2)}) %collective-permute-start.3) | collective-permute-done | bytes 16160 | tf_op jit(solution)/shard_map/ppermute | solution.py:611
  30.4 0.8 concatenate.21.parts
  31.3 47.6 %shard_map.141 = (f32[112,768]{1,0:T(8,128)}, s32[112,128]{1,0:T(8,128)}, s32[16,128]{1,0:T(8,128)}, f32[8,768]{1,0:T(8,128)}) custom-call(f32[112,768]{1,0:T(8,128)} %concatenate.21.parts, s32[8,768]{1,0:T(8,128)} %constant.4.clone.coord, s32[8,768]{1,0:T(8,128)} %constant.12.clone.source, f32[3,16,4,4,256]{4,3,2,1,0:T(4,128)} %pos.5, ...), custom_call_target="tpu_custom_call" | custom-call | tf_op jit(solution)/shard_map/pallas_call | solution.py:564
  79.7 5.1 %collective-permute-start.6 = (f32[8,72]{1,0:T(8,128)S(1)}, f32[8,72]{1,0:T(8,128)S(1)}, u32[]{:S(2)}, u32[]{:S(2)}) collective-permute-start(f32[8,72]{1,0:T(8,128)S(1)} %get-tuple-element.33), channel_id=1, source_target_pairs={{0,124},{4,0},{8,4},{12,8},{16,12},{20,16},{24,20},{28,24},{32,28}... | collective-permute-start | bytes 6920 | tf_op jit(solution)/shard_map/ppermute | solution.py:632
  86.3 1.6 collective-permute-start.9
  87.9 3.1 %collective-permute-start.7 = (f32[8,768]{1,0:T(8,128)S(1)}, f32[8,768]{1,0:T(8,128)S(1)}, u32[]{:S(2)}, u32[]{:S(2)}) collective-permute-start(f32[8,768]{1,0:T(8,128)S(1)} %pad_maximum_fusion.2.fresh), channel_id=1, source_target_pairs={{0,2},{1,3},{2,0},{3,1},{4,6},{5,7},{6,4},{7,5},{8,10},{9,11},{10,... | collective-permute-start | bytes 73736 | tf_op jit(solution)/shard_map/ppermute | solution.py:625
  91.9 1.3 collective-permute-done.7.fresh_y
  93.9 96.6 %shard_map.142 = (f32[24,768]{1,0:T(8,128)}, f32[16,4,4,256]{3,2,1,0:T(4,128)}) custom-call(f32[112,768]{1,0:T(8,128)} %get-tuple-element.12.table, f32[8,768]{1,0:T(8,128)} %copy-done.4, f32[8,768]{1,0:T(8,128)} %copy-done.12, f32[8,768]{1,0:T(8,128)} %copy-done.11, f32[8,768]{1,0:T(8,128)} %copy-done.10, s32[112,128]{1,0:T(8,128)} %get-tuple-element.14.list_v, ...), custom_call_target="tpu_custom_call" | custom-call | tf_op jit(solution)/shard_map/pallas_call | solution.py:564
  191.3 2.1 collective-permute-start.11
  193.4 1.4 collective-permute-done.11
  194.8 0.9 slice_add_fusion
  195.9 6.3 %collective-permute-done.10 = f32[24,36]{1,0:T(8,128)S(1)} collective-permute-done((f32[24,36]{1,0:T(8,128)S(1)}, f32[24,36]{1,0:T(8,128)S(1)}, u32[]{:S(2)}, u32[]{:S(2)}) %collective-permute-start.10) | collective-permute-done | bytes 3488 | tf_op jit(solution)/shard_map/ppermute | solution.py:642
  202.4 3.3 %collective-permute-start.14 = (f32[24,768]{1,0:T(8,128)S(1)}, f32[24,768]{1,0:T(8,128)S(1)}, u32[]{:S(2)}, u32[]{:S(2)}) collective-permute-start(f32[24,768]{1,0:T(8,128)S(1)} %concatenate.23.pushed), channel_id=1, source_target_pairs={{0,3},{1,2},{2,1},{3,0},{4,7},{5,6},{6,5},{7,4},{8,11},{9,10},{10,... | collective-permute-start | bytes 221192 | tf_op jit(solution)/shard_map/ppermute | solution.py:625
  205.6 2.7 %collective-permute-start.13 = (f32[24,768]{1,0:T(8,128)S(1)}, f32[24,768]{1,0:T(8,128)S(1)}, u32[]{:S(2)}, u32[]{:S(2)}) collective-permute-start(f32[24,768]{1,0:T(8,128)S(1)} %concatenate.23.pushed), channel_id=1, source_target_pairs={{0,1},{1,0},{2,3},{3,2},{4,5},{5,4},{6,7},{7,6},{8,9},{9,8},{10,11... | collective-permute-start | bytes 221192 | tf_op jit(solution)/shard_map/ppermute | solution.py:625
  208.6 2.1 collective-permute-done.13.pushed_z
  210.7 3.5 %collective-permute-done.12.pushed_y = f32[24,768]{1,0:T(8,128)S(1)} collective-permute-done((f32[24,768]{1,0:T(8,128)S(1)}, f32[24,768]{1,0:T(8,128)S(1)}, u32[]{:S(2)}, u32[]{:S(2)}) %collective-permute-start.12) | collective-permute-done | bytes 73760 | tf_op jit(solution)/shard_map/ppermute | solution.py:625
  214.8 3.7 %shard_map.143 = f32[3,16,4,4,256]{4,3,2,1,0:T(4,128)} custom-call(f32[24,768]{1,0:T(8,128)} %copy-done.1, f32[24,768]{1,0:T(8,128)} %copy-done.7, f32[24,768]{1,0:T(8,128)} %copy-done.6, f32[24,768]{1,0:T(8,128)} %copy-done.5, s32[8,768]{1,0:T(8,128)} %constant.4.clone.coord, s32[8,256]{1,0:T(8,128)} %constant.13.clone.home, s32[256,1]{1,0:T(8,128)} %reshape.29.active), custom_call_target="tpu_custom_call" | custom-call | tf_op jit(solution)/shard_map/pallas_call | solution.py:564
  (71 shorter events, 10.3 us)
Async XLA Ops:
  8.1 5.6 %copy-start = (f32[112,256]{1,0:T(8,128)S(1)}, f32[112,256]{1,0:T(8,128)}, u32[]{:S(2)}) copy-start(f32[112,256]{1,0:T(8,128)} %get-tuple-element.10) | copy-start | bytes 344068
  8.1 10.8 %collective-permute-start.1 = (f32[112,128]{1,0:T(8,128)S(1)}, f32[112,128]{1,0:T(8,128)S(1)}, u32[]{:S(2)}, u32[]{:S(2)}) collective-permute-start(f32[112,128]{1,0:T(8,128)S(1)} %get-tuple-element.18), channel_id=1, source_target_pairs={{0,1},{1,0},{2,3},{3,2},{4,5},{5,4},{6,7},{7,6},{8,9},{9,8},{10,11... | collective-permute-start | bytes 172040 | tf_op jit(solution)/shard_map/ppermute | solution.py:606
  9.7 9.0 %collective-permute-start = (f32[112,128]{1,0:T(8,128)S(1)}, f32[112,128]{1,0:T(8,128)S(1)}, u32[]{:S(2)}, u32[]{:S(2)}) collective-permute-start(f32[112,128]{1,0:T(8,128)S(1)} %get-tuple-element.19), channel_id=1, source_target_pairs={{0,2},{1,3},{2,0},{3,1},{4,6},{5,7},{6,4},{7,5},{8,10},{9,11},{10,... | collective-permute-start | bytes 172040 | tf_op jit(solution)/shard_map/ppermute | solution.py:606
  13.3 5.4 %collective-permute-start.2 = (f32[112,64]{1,0:T(8,128)S(1)}, f32[112,64]{1,0:T(8,128)S(1)}, u32[]{:S(2)}, u32[]{:S(2)}) collective-permute-start(f32[112,64]{1,0:T(8,128)S(1)} %slice.68), channel_id=1, source_target_pairs={{0,3},{1,2},{2,1},{3,0},{4,7},{5,6},{6,5},{7,4},{8,11},{9,10},{10,... | collective-permute-start | bytes 86024 | tf_op jit(solution)/shard_map/ppermute | solution.py:606
  19.0 6.1 %collective-permute-start.4 = (f32[112,36]{1,0:T(8,128)S(1)}, f32[112,36]{1,0:T(8,128)S(1)}, u32[]{:S(2)}, u32[]{:S(2)}) collective-permute-start(f32[112,36]{1,0:T(8,128)S(1)} %pad_maximum_fusion.1), channel_id=1, source_target_pairs={{0,124},{4,0},{8,4},{12,8},{16,12},{20,16},{24,20},{28,24},{32,28}... | collective-permute-start | bytes 48392 | tf_op jit(solution)/shard_map/ppermute | solution.py:612
  23.4 7.0 %collective-permute-start.3 = (f32[112,36]{1,0:T(8,128)S(1)}, f32[112,36]{1,0:T(8,128)S(1)}, u32[]{:S(2)}, u32[]{:S(2)}) collective-permute-start(f32[112,36]{1,0:T(8,128)S(1)} %pad_maximum_fusion), channel_id=1, source_target_pairs={{0,4},{4,8},{8,12},{12,16},{16,20},{20,24},{24,28},{28,32},{32,36}... | collective-permute-start | bytes 48392 | tf_op jit(solution)/shard_map/ppermute | solution.py:611
  78.9 6.7 %copy-start.8 = (f32[8,768]{1,0:T(8,128)S(1)}, f32[8,768]{1,0:T(8,128)}, u32[]{:S(2)}) copy-start(f32[8,768]{1,0:T(8,128)} %get-tuple-element.13) | copy-start | bytes 73732
  79.7 6.4 %collective-permute-start.5 = (f32[8,72]{1,0:T(8,128)S(1)}, f32[8,72]{1,0:T(8,128)S(1)}, u32[]{:S(2)}, u32[]{:S(2)}) collective-permute-start(f32[8,72]{1,0:T(8,128)S(1)} %get-tuple-element.32), channel_id=1, source_target_pairs={{0,4},{4,8},{8,12},{12,16},{16,20},{20,24},{24,28},{28,32},{32,36}... | collective-permute-start | bytes 6920 | tf_op jit(solution)/shard_map/ppermute | solution.py:631
  79.7 6.4 %collective-permute-start.6 = (f32[8,72]{1,0:T(8,128)S(1)}, f32[8,72]{1,0:T(8,128)S(1)}, u32[]{:S(2)}, u32[]{:S(2)}) collective-permute-start(f32[8,72]{1,0:T(8,128)S(1)} %get-tuple-element.33), channel_id=1, source_target_pairs={{0,124},{4,0},{8,4},{12,8},{16,12},{20,16},{24,20},{28,24},{32,28}... | collective-permute-start | bytes 6920 | tf_op jit(solution)/shard_map/ppermute | solution.py:632
  86.2 4.8 %copy-start.9 = (s32[16,4,4]{0,2,1:T(4,128)S(1)}, s32[16,4,4]{0,2,1:T(4,128)}, u32[]{:S(2)}) copy-start(s32[16,4,4]{0,2,1:T(4,128)} %param.20) | copy-start | bytes 3076
  86.3 5.6 %copy-start.4 = (f32[8,768]{1,0:T(8,128)}, f32[8,768]{1,0:T(8,128)S(1)}, u32[]{:S(2)}) copy-start(f32[8,768]{1,0:T(8,128)S(1)} %pad_maximum_fusion.2.fresh) | copy-start | bytes 73732
  86.3 5.6 %collective-permute-start.9 = (f32[8,768]{1,0:T(8,128)S(1)}, f32[8,768]{1,0:T(8,128)S(1)}, u32[]{:S(2)}, u32[]{:S(2)}) collective-permute-start(f32[8,768]{1,0:T(8,128)S(1)} %pad_maximum_fusion.2.fresh), channel_id=1, source_target_pairs={{0,3},{1,2},{2,1},{3,0},{4,7},{5,6},{6,5},{7,4},{8,11},{9,10},{10,... | collective-permute-start | bytes 73736 | tf_op jit(solution)/shard_map/ppermute | solution.py:625
  87.9 4.0 %collective-permute-start.8 = (f32[8,768]{1,0:T(8,128)S(1)}, f32[8,768]{1,0:T(8,128)S(1)}, u32[]{:S(2)}, u32[]{:S(2)}) collective-permute-start(f32[8,768]{1,0:T(8,128)S(1)} %pad_maximum_fusion.2.fresh), channel_id=1, source_target_pairs={{0,1},{1,0},{2,3},{3,2},{4,5},{5,4},{6,7},{7,6},{8,9},{9,8},{10,11... | collective-permute-start | bytes 73736 | tf_op jit(solution)/shard_map/ppermute | solution.py:625
  87.9 5.3 %collective-permute-start.7 = (f32[8,768]{1,0:T(8,128)S(1)}, f32[8,768]{1,0:T(8,128)S(1)}, u32[]{:S(2)}, u32[]{:S(2)}) collective-permute-start(f32[8,768]{1,0:T(8,128)S(1)} %pad_maximum_fusion.2.fresh), channel_id=1, source_target_pairs={{0,2},{1,3},{2,0},{3,1},{4,6},{5,7},{6,4},{7,5},{8,10},{9,11},{10,... | collective-permute-start | bytes 73736 | tf_op jit(solution)/shard_map/ppermute | solution.py:625
  91.9 1.4 copy-start.10
  190.5 5.2 %copy-start.2 = (f32[24,768]{1,0:T(8,128)S(1)}, f32[24,768]{1,0:T(8,128)}, u32[]{:S(2)}) copy-start(f32[24,768]{1,0:T(8,128)} %get-tuple-element.17) | copy-start | bytes 221188
  191.3 3.5 %collective-permute-start.11 = (f32[24,36]{1,0:T(8,128)S(1)}, f32[24,36]{1,0:T(8,128)S(1)}, u32[]{:S(2)}, u32[]{:S(2)}) collective-permute-start(f32[24,36]{1,0:T(8,128)S(1)} %slice.81), channel_id=1, source_target_pairs={{0,124},{4,0},{8,4},{12,8},{16,12},{20,16},{24,20},{28,24},{32,28}... | collective-permute-start | bytes 10376 | tf_op jit(solution)/shard_map/ppermute | solution.py:643
  195.7 6.4 %collective-permute-start.10 = (f32[24,36]{1,0:T(8,128)S(1)}, f32[24,36]{1,0:T(8,128)S(1)}, u32[]{:S(2)}, u32[]{:S(2)}) collective-permute-start(f32[24,36]{1,0:T(8,128)S(1)} %get-tuple-element.23), channel_id=1, source_target_pairs={{0,4},{4,8},{8,12},{12,16},{16,20},{20,24},{24,28},{28,32},{32,36}... | collective-permute-start | bytes 10376 | tf_op jit(solution)/shard_map/ppermute | solution.py:642
  202.4 11.8 %copy-start.1 = (f32[24,768]{1,0:T(8,128)}, f32[24,768]{1,0:T(8,128)S(1)}, u32[]{:S(2)}) copy-start(f32[24,768]{1,0:T(8,128)S(1)} %concatenate.23.pushed) | copy-start | bytes 221188
  202.4 6.2 %collective-permute-start.14 = (f32[24,768]{1,0:T(8,128)S(1)}, f32[24,768]{1,0:T(8,128)S(1)}, u32[]{:S(2)}, u32[]{:S(2)}) collective-permute-start(f32[24,768]{1,0:T(8,128)S(1)} %concatenate.23.pushed), channel_id=1, source_target_pairs={{0,3},{1,2},{2,1},{3,0},{4,7},{5,6},{6,5},{7,4},{8,11},{9,10},{10,... | collective-permute-start | bytes 221192 | tf_op jit(solution)/shard_map/ppermute | solution.py:625
  205.6 5.0 %collective-permute-start.13 = (f32[24,768]{1,0:T(8,128)S(1)}, f32[24,768]{1,0:T(8,128)S(1)}, u32[]{:S(2)}, u32[]{:S(2)}) collective-permute-start(f32[24,768]{1,0:T(8,128)S(1)} %concatenate.23.pushed), channel_id=1, source_target_pairs={{0,1},{1,0},{2,3},{3,2},{4,5},{5,4},{6,7},{7,6},{8,9},{9,8},{10,11... | collective-permute-start | bytes 221192 | tf_op jit(solution)/shard_map/ppermute | solution.py:625
  208.3 5.9 %collective-permute-start.12 = (f32[24,768]{1,0:T(8,128)S(1)}, f32[24,768]{1,0:T(8,128)S(1)}, u32[]{:S(2)}, u32[]{:S(2)}) collective-permute-start(f32[24,768]{1,0:T(8,128)S(1)} %concatenate.23.pushed), channel_id=1, source_target_pairs={{0,2},{1,3},{2,0},{3,1},{4,6},{5,7},{6,4},{7,5},{8,10},{9,11},{10,... | collective-permute-start | bytes 221192 | tf_op jit(solution)/shard_map/ppermute | solution.py:625
  208.6 5.6 %copy-start.5 = (f32[24,768]{1,0:T(8,128)}, f32[24,768]{1,0:T(8,128)S(1)}, u32[]{:S(2)}) copy-start(f32[24,768]{1,0:T(8,128)S(1)} %collective-permute-done.14.pushed_yz) | copy-start | bytes 221188
  210.7 3.5 %copy-start.6 = (f32[24,768]{1,0:T(8,128)}, f32[24,768]{1,0:T(8,128)S(1)}, u32[]{:S(2)}) copy-start(f32[24,768]{1,0:T(8,128)S(1)} %collective-permute-done.13.pushed_z) | copy-start | bytes 221188
  (5 other events, 4.6 us)

commit v3 on v2

--- a/solution.py
+++ b/solution.py
@@ -86,12 +86,15 @@
 
 
 def picked(values, source_row):
-    size = values.shape[1]
+    count, size = values.shape
     rows = lax.broadcasted_iota(i32, (size, source_row.shape[1]), 0)
-    chosen = (rows == source_row).astype(f32)
-    return lax.dot_general(
-        values, chosen, (((1,), (0,)), ((), ())), precision=HIGHEST, preferred_element_type=f32
-    )
+    chosen = (rows == source_row).astype(f32).astype(jnp.bfloat16)
+    high = values.astype(jnp.bfloat16).astype(f32)
+    rest = values - high
+    middle = rest.astype(jnp.bfloat16).astype(f32)
+    parts = jnp.concatenate([high, middle, rest - middle], 0).astype(jnp.bfloat16)
+    out = jnp.dot(parts, chosen, preferred_element_type=f32)
+    return out[:count] + out[count : 2 * count] + out[2 * count :]
 
 
 def unit_rows():
@@ -118,7 +121,7 @@
     return jnp.where(slot < count, mass, 0.0)
 
 
-def pack_kernel(pos, vel, mass, smooth, entropy, stored, count, flags, sent, table, faces):
+def pack_kernel(pos, vel, mass, smooth, entropy, stored, count, flags, sent, table, y_part, z_part, edge, low, high):
     fields = [pos[c].reshape(CELLS, 256) for c in range(3)]
     fields.append(live_mass(mass[...].reshape(CELLS, 256), count[...]))
     fields.append(smooth[...].reshape(CELLS, 256))
@@ -127,7 +130,12 @@
     for f, field in enumerate(fields):
         table[8 * f : 8 * f + 8, :] = cells_to_lanes(field)
     table[FLAGS:ROWS, :] = flags[...]
-    faces[...] = picked(table[...], sent[0:1, :])
+    faces = picked(table[...], sent[0:1, :])
+    y_part[...] = faces[:, :128]
+    z_part[...] = faces[:, 128:256]
+    edge[...] = faces[:, 256:320]
+    low[...] = table[:, :16]
+    high[...] = table[:, CELLS - 16 :]
 
 
 def segment_units():
@@ -166,16 +174,26 @@
 
 
 def build_lists(table, coord, list_d, list_f, count_d, count_f):
-    active = lax.broadcasted_iota(i32, (8, LANES), 0).astype(f32) < table[LIVE : LIVE + 1, :]
+    row = lax.broadcasted_iota(i32, (8, LANES), 0)
+    active = row.astype(f32) < table[LIVE : LIVE + 1, :]
     reach = 4.0 * table[32:40, :] * table[32:40, :] * 1.0001
-    squares = []
-    for c in range(3):
+    for_density = row % 4 == 3
+    far = jnp.where(active, 0.0, 1e9)
+    squares, inside, cells = [], [], []
+    for c, (extent, step) in enumerate(((BX, BY * BZ), (BY, BZ), (BZ, 1))):
         p = table[8 * c : 8 * c + 8, :]
-        squares.append({-1: p * p, 0: None, 1: (1.0 - p) * (1.0 - p)})
-    far = jnp.where(active, 0.0, 1e9)
-    cx, cy, cz = coord[0:1, :], coord[1:2, :], coord[2:3, :]
-    entries_d, entries_f = [], []
-    kept_d = kept_f = jnp.zeros((2, LANES), i32)
+        squares.append({-1: p * p, 1: (1.0 - p) * (1.0 - p)})
+        at = jnp.broadcast_to(coord[c : c + 1, :], (8, LANES))
+        inside.append({o: (at + o >= 0) & (at + o < extent) for o in (-1, 0, 1)})
+        cells.append(at * step)
+    base = cells[0] + cells[1] + cells[2]
+
+    def nearest(values):
+        values = jnp.minimum(values, pltpu.roll(values, 1, 0))
+        return jnp.minimum(values, pltpu.roll(values, 2, 0))
+
+    entries = []
+    kept = jnp.zeros((8, LANES), i32)
     center = 13
     offsets = OFFSETS[:center] + [(0, 0, 0)] + OFFSETS[center:]
     for k, (ox, oy, oz) in enumerate(offsets):
@@ -183,55 +201,43 @@
         for c, o in enumerate((ox, oy, oz)):
             if o:
                 away = away + squares[c][o]
-        bx, by, bz = cx + ox, cy + oy, cz + oz
-        ok = (bx >= 0) & (bx < BX) & (by >= 0) & (by < BY) & (bz >= 0) & (bz < BZ)
+        keep = inside[0][ox] & inside[1][oy] & inside[2][oz]
         if k != center:
-            row = FLAGS + (k if k < center else k - 1)
-            ok = ok & (table[row : row + 1, :] > 0.5)
-        cell = (bx * BY + by) * BZ + bz
-        over_d = away - reach
-        over_f = away - 1.0001
-
-        def near(over):
-            return jnp.concatenate(
-                [jnp.min(over[0:4], 0, keepdims=True), jnp.min(over[4:8], 0, keepdims=True)], 0
-            )
-
-        both = jnp.concatenate([cell, cell], 0)
-        oks = jnp.concatenate([ok.astype(i32), ok.astype(i32)], 0) > 0
-        for over, entries, which in ((over_d, entries_d, 0), (over_f, entries_f, 1)):
-            keep = oks & (near(over) <= 0.0)
-            kept = kept_d if which == 0 else kept_f
-            entries.append(jnp.where(keep, both + (k - kept) * 1024, NONE))
-            if which == 0:
-                kept_d = kept + keep.astype(i32)
-            else:
-                kept_f = kept + keep.astype(i32)
-    for entries, target, kept, counted in (
-        (entries_d, list_d, kept_d, count_d), (entries_f, list_f, kept_f, count_f),
-    ):
-        for bit in range(5):
-            step, mask = 1 << bit, 1024 << bit
-            moves = [(e & mask) != 0 for e in entries]
-            moved = []
-            for p in range(27):
-                e = jnp.where(moves[p], NONE, entries[p])
-                if p + step < 27:
-                    e = jnp.where(moves[p + step], entries[p + step], e)
-                moved.append(e)
-            entries = moved
-        entries = [e & 1023 for e in entries]
-        for p in range(WORDS):
-            word = entries[3 * p] + (entries[3 * p + 1] << 10) + (entries[3 * p + 2] << 20)
-            for group in range(2):
-                for t in range(TILES):
-                    at = (p * 2 + group) * TILES + t
-                    target[at : at + 1, :] = word[group : group + 1, 128 * t : 128 * t + 128]
+            flag = FLAGS + (k if k < center else k - 1)
+            keep = keep & (table[flag : flag + 1, :] > 0.5)
+        over = jnp.where(
+            for_density, nearest(away - reach), pltpu.roll(nearest(away - 1.0001), 7, 0)
+        )
+        keep = keep & (over <= 0.0)
+        cell = base + ((ox * BY + oy) * BZ + oz + k * 1024)
+        entries.append(jnp.where(keep, cell - kept * 1024, NONE))
+        kept = kept + keep.astype(i32)
+    for bit in range(5):
+        step, mask = 1 << bit, 1024 << bit
+        moves = [(e & mask) != 0 for e in entries]
+        moved = []
+        for p in range(27):
+            e = jnp.where(moves[p], NONE, entries[p])
+            if p + step < 27:
+                e = jnp.where(moves[p + step], entries[p + step], e)
+            moved.append(e)
+        entries = moved
+    entries = [e & 1023 for e in entries]
+    for p in range(WORDS):
+        word = entries[3 * p] + (entries[3 * p + 1] << 10) + (entries[3 * p + 2] << 20)
+        for group in range(2):
+            for t in range(TILES):
+                at = (p * 2 + group) * TILES + t
+                for first, target in ((3, list_d), (2, list_f)):
+                    target[at : at + 1, :] = word[
+                        first + 4 * group : first + 4 * group + 1, 128 * t : 128 * t + 128
+                    ]
+    for first, target, counted in ((3, list_d, count_d), (2, list_f, count_f)):
         target[WORDS * 2 * TILES :, :] = jnp.full((LIST_ROWS - WORDS * 2 * TILES, 128), NONE, i32)
         for group in range(2):
             for t in range(TILES):
                 counted[group * TILES + t : group * TILES + t + 1, :] = kept[
-                    group : group + 1, 128 * t : 128 * t + 128
+                    first + 4 * group : first + 4 * group + 1, 128 * t : 128 * t + 128
                 ]
         counted[2 * TILES :, :] = jnp.zeros((16 - 2 * TILES, 128), i32)
 
@@ -296,21 +302,22 @@
 
 def run_items(total, batch, items, lists, item, add):
     per_row = 128 // batch
+    bits = per_row.bit_length() - 1
 
     def take(turn):
-        codes = [items[turn // per_row, (turn % per_row) * batch + u] for u in range(batch)]
+        row, start = turn >> bits, (turn & (per_row - 1)) * batch
+        codes = [items[row, start + u] for u in range(batch)]
         return codes, [lists[code >> 18, (code >> 11) & 127] for code in codes]
 
     def step(turn, carry):
         codes, words = carry
-        later = take(turn + 1)
         results = []
         for code, word in zip(codes, words):
             group = code & 2047
             results.append((group, item(group, (word & 1023, (word >> 10) & 1023, word >> 20))))
         for group, values in results:
             add(group, values)
-        return later
+        return take(turn + 1)
 
     lax.fori_loop(0, (total + batch - 1) // batch, step, take(jnp.int32(0)))
 
@@ -600,14 +607,13 @@
     return [(i, (i + by) % devices) for i in range(devices)]
 
 
-def first_exchange(table, faces):
-    y_part, z_part, edge = faces[:, :128], faces[:, 128:256], faces[:, 256:320]
+def first_exchange(table, y_part, z_part, edge, low, high):
     y_in, z_in, edge_in = (
         lax.ppermute(part, ("gy", "gz"), pairs)
         for part, pairs in zip((y_part, z_part, edge), ACROSS)
     )
-    low = jnp.concatenate([table[:, :16], y_in[:, :8], z_in[:, :8], edge_in[:, :4]], 1)
-    high = jnp.concatenate([table[:, 240:], y_in[:, 120:], z_in[:, 120:], edge_in[:, 60:]], 1)
+    low = jnp.concatenate([low, y_in[:, :8], z_in[:, :8], edge_in[:, :4]], 1)
+    high = jnp.concatenate([high, y_in[:, 120:], z_in[:, 120:], edge_in[:, 60:]], 1)
     before = lax.ppermute(high, "gx", ring("gx", 1))
     after = lax.ppermute(low, "gx", ring("gx", -1))
     unused = jnp.zeros((ROWS, LANES - EXT), f32)
@@ -668,8 +674,8 @@
         0,
     )
     inputs = (pos, vel, mass, smooth, entropy, stored, count, flags, jnp.asarray(sent_cells()))
-    table, faces = call(pack_kernel, inputs, [shape(ROWS, CELLS), shape(ROWS, 384)])
-    parts = first_exchange(table, faces)
+    widths = (CELLS, 128, 128, 64, 16, 16)
+    parts = first_exchange(*call(pack_kernel, inputs, [shape(ROWS, width) for width in widths]))
     inputs = (parts, coord, source, pos, mass, count)
     table, list_f, count_f, sums = call(
         density_kernel,

time: 219 us -> 201 us (0.918)
  Pallas kernels: 152 us -> 136 us
    pallas_call x4, Pallas kernels: 152 us -> 136 us  [call(): pl.pallas_call(kernel, out_shape=outputs, in_specs=in_specs or [VMEM_SPEC...]
  transfers between devices with their start and end apart: 15 -> 15, of which waited for: 9 -> 11; matrix products, arithmetic and copies ran while one was open for 1% -> 1% of each run, Pallas kernels for 0% -> 0%
where the time goes in v3:
time: 201 us; the launch traced here: 200 us
  Pallas kernels  136 us (68%)
  starting transfers between devices  26.9 us (13%)
  waiting for transfers between devices  26.4 us (13%)
  local copies, waits for them, and re-layouts  7.26 us (4%)
  other arithmetic  2.75 us (1%)
    pallas_call x4, Pallas kernels, call(): pl.pallas_call(kernel, out_shape=outputs, in_specs=in_specs or [VMEM_SPEC...  136 us
    ppermute x6, starting transfers between devices, sent_across(): return [lax.ppermute(sums, ('gy', 'gz'), pairs) for pairs in ACROSS]  11.5 us
    ppermute x6, waiting for transfers between devices, sent_across(): return [lax.ppermute(sums, ('gy', 'gz'), pairs) for pairs in ACROSS]  6.81 us
    ppermute x1, waiting for transfers between devices, returned_sums(): before = lax.ppermute(sums[:, top + plane:EXT], 'gx', ring('gx', 1))  6.27 us
    ppermute x1, waiting for transfers between devices, first_exchange(): before = lax.ppermute(high, 'gx', ring('gx', 1))  5.29 us
    ppermute x1, starting transfers between devices, shared_sums(): after = lax.ppermute(sums[:, :2 * plane], 'gx', ring('gx', -1))  5.06 us
    ppermute x1, starting transfers between devices, first_exchange(): after = lax.ppermute(low, 'gx', ring('gx', -1))  4.7 us
    ppermute x3, waiting for transfers between devices, first_exchange(): lax.ppermute(part, ('gy', 'gz'), pairs)  4.48 us
  transfers between devices with their start and end apart: 15, of which 11 were waited for; matrix products, arithmetic and copies ran while one was open for 1% of the time, Pallas kernels for 0%

profile of v3, /device:TPU:0, one launch (start us, length us, event | category | flops | bytes accessed | tf_op | source)
XLA Modules:
  0.0 199.7 jit_solution(7375585102233567749)
XLA Ops:
  3.3 3.7 %shard_map.140 = (f32[112,256]{1,0:T(8,128)}, f32[112,128]{1,0:T(8,128)}, f32[112,128]{1,0:T(8,128)}, f32[112,64]{1,0:T(8,128)}, f32[112,16]{1,0:T(8,128)}, /*index=5*/f32[112,16]{1,0:T(8,128)}) custom-call(f32[3,16,4,4,256]{4,3,2,1,0:T(4,128)} %pos.5, f32[3,16,4,4,256]{4,3,2,1,0:T(4,128)} %vel.3, f32[16,4,4,256]{3,2,1,0:T(4,128)} %mass.5, ...), custom_call_target="tpu_custom_call" | custom-call | tf_op jit(solution)/shard_map/pallas_call | solution.py:571
  7.1 2.8 %collective-permute-start.2 = (f32[112,64]{1,0:T(8,128)}, f32[112,64]{1,0:T(8,128)S(1)}, u32[]{:S(2)}, u32[]{:S(2)}) collective-permute-start(f32[112,64]{1,0:T(8,128)} %get-tuple-element.17), channel_id=1, source_target_pairs={{0,3},{1,2},{2,1},{3,0},{4,7},{5,6},{6,5},{7,4},{8,11},{9,10},{10,... | collective-permute-start | bytes 86024 | tf_op jit(solution)/shard_map/ppermute | solution.py:612
  9.9 0.8 collective-permute-start
  11.2 1.5 collective-permute-done.2
  12.7 2.4 %collective-permute-done.1 = f32[112,128]{1,0:T(8,128)S(1)} collective-permute-done((f32[112,128]{1,0:T(8,128)}, f32[112,128]{1,0:T(8,128)S(1)}, u32[]{:S(2)}, u32[]{:S(2)}) %collective-permute-start.1) | collective-permute-done | bytes 57376 | tf_op jit(solution)/shard_map/ppermute | solution.py:612
  16.1 4.7 %collective-permute-start.4 = (f32[112,36]{1,0:T(8,128)S(1)}, f32[112,36]{1,0:T(8,128)S(1)}, u32[]{:S(2)}, u32[]{:S(2)}) collective-permute-start(f32[112,36]{1,0:T(8,128)S(1)} %pad_maximum_fusion.1), channel_id=1, source_target_pairs={{0,124},{4,0},{8,4},{12,8},{16,12},{20,16},{24,20},{28,24},{32,28}... | collective-permute-start | bytes 48392 | tf_op jit(solution)/shard_map/ppermute | solution.py:618
  21.0 1.6 collective-permute-done.4
  22.6 5.3 %collective-permute-done.3 = f32[112,36]{1,0:T(8,128)S(1)} collective-permute-done((f32[112,36]{1,0:T(8,128)S(1)}, f32[112,36]{1,0:T(8,128)S(1)}, u32[]{:S(2)}, u32[]{:S(2)}) %collective-permute-start.3) | collective-permute-done | bytes 16160 | tf_op jit(solution)/shard_map/ppermute | solution.py:617
  27.9 0.8 concatenate.21.parts
  28.8 40.2 %shard_map.141 = (f32[112,768]{1,0:T(8,128)}, s32[112,128]{1,0:T(8,128)}, s32[16,128]{1,0:T(8,128)}, f32[8,768]{1,0:T(8,128)}) custom-call(f32[112,768]{1,0:T(8,128)} %concatenate.21.parts, s32[8,768]{1,0:T(8,128)} %constant.4.clone.coord, s32[8,768]{1,0:T(8,128)} %constant.12.clone.source, f32[3,16,4,4,256]{4,3,2,1,0:T(4,128)} %pos.5, ...), custom_call_target="tpu_custom_call" | custom-call | tf_op jit(solution)/shard_map/pallas_call | solution.py:571
  69.0 0.8 fusion.3
  69.9 5.1 %collective-permute-start.6 = (f32[8,72]{1,0:T(8,128)S(1)}, f32[8,72]{1,0:T(8,128)S(1)}, u32[]{:S(2)}, u32[]{:S(2)}) collective-permute-start(f32[8,72]{1,0:T(8,128)S(1)} %get-tuple-element.37), channel_id=1, source_target_pairs={{0,124},{4,0},{8,4},{12,8},{16,12},{20,16},{24,20},{28,24},{32,28}... | collective-permute-start | bytes 6920 | tf_op jit(solution)/shard_map/ppermute | solution.py:638
  77.5 3.6 %collective-permute-start.7 = (f32[8,768]{1,0:T(8,128)S(1)}, f32[8,768]{1,0:T(8,128)S(1)}, u32[]{:S(2)}, u32[]{:S(2)}) collective-permute-start(f32[8,768]{1,0:T(8,128)S(1)} %pad_maximum_fusion.2.fresh), channel_id=1, source_target_pairs={{0,2},{1,3},{2,0},{3,1},{4,6},{5,7},{6,4},{7,5},{8,10},{9,11},{10,... | collective-permute-start | bytes 73736 | tf_op jit(solution)/shard_map/ppermute | solution.py:631
  82.0 1.2 collective-permute-done.7.fresh_y
  83.8 88.8 %shard_map.142 = (f32[24,768]{1,0:T(8,128)}, f32[16,4,4,256]{3,2,1,0:T(4,128)}) custom-call(f32[112,768]{1,0:T(8,128)} %get-tuple-element.20.table, f32[8,768]{1,0:T(8,128)} %copy-done.4, f32[8,768]{1,0:T(8,128)} %copy-done.14, f32[8,768]{1,0:T(8,128)} %copy-done.13, f32[8,768]{1,0:T(8,128)} %copy-done.12, s32[112,128]{1,0:T(8,128)} %get-tuple-element.22.list_v, ...), custom_call_target="tpu_custom_call" | custom-call | tf_op jit(solution)/shard_map/pallas_call | solution.py:571
  173.4 1.4 collective-permute-start.11
  174.8 1.4 collective-permute-done.11
  176.2 0.9 slice_add_fusion
  177.3 6.3 %collective-permute-done.10 = f32[24,36]{1,0:T(8,128)S(1)} collective-permute-done((f32[24,36]{1,0:T(8,128)S(1)}, f32[24,36]{1,0:T(8,128)S(1)}, u32[]{:S(2)}, u32[]{:S(2)}) %collective-permute-start.10) | collective-permute-done | bytes 3488 | tf_op jit(solution)/shard_map/ppermute | solution.py:648
  183.8 3.8 %collective-permute-start.14 = (f32[24,768]{1,0:T(8,128)S(1)}, f32[24,768]{1,0:T(8,128)S(1)}, u32[]{:S(2)}, u32[]{:S(2)}) collective-permute-start(f32[24,768]{1,0:T(8,128)S(1)} %concatenate.23.pushed), channel_id=1, source_target_pairs={{0,3},{1,2},{2,1},{3,0},{4,7},{5,6},{6,5},{7,4},{8,11},{9,10},{10,... | collective-permute-start | bytes 221192 | tf_op jit(solution)/shard_map/ppermute | solution.py:631
  187.6 2.7 %collective-permute-start.13 = (f32[24,768]{1,0:T(8,128)S(1)}, f32[24,768]{1,0:T(8,128)S(1)}, u32[]{:S(2)}, u32[]{:S(2)}) collective-permute-start(f32[24,768]{1,0:T(8,128)S(1)} %concatenate.23.pushed), channel_id=1, source_target_pairs={{0,1},{1,0},{2,3},{3,2},{4,5},{5,4},{6,7},{7,6},{8,9},{9,8},{10,11... | collective-permute-start | bytes 221192 | tf_op jit(solution)/shard_map/ppermute | solution.py:631
  190.5 2.1 %collective-permute-done.13.pushed_z = f32[24,768]{1,0:T(8,128)S(1)} collective-permute-done((f32[24,768]{1,0:T(8,128)S(1)}, f32[24,768]{1,0:T(8,128)S(1)}, u32[]{:S(2)}, u32[]{:S(2)}) %collective-permute-start.13) | collective-permute-done | bytes 73760 | tf_op jit(solution)/shard_map/ppermute | solution.py:631
  192.6 3.5 %collective-permute-done.12.pushed_y = f32[24,768]{1,0:T(8,128)S(1)} collective-permute-done((f32[24,768]{1,0:T(8,128)S(1)}, f32[24,768]{1,0:T(8,128)S(1)}, u32[]{:S(2)}, u32[]{:S(2)}) %collective-permute-start.12) | collective-permute-done | bytes 73760 | tf_op jit(solution)/shard_map/ppermute | solution.py:631
  196.8 3.0 %shard_map.143 = f32[3,16,4,4,256]{4,3,2,1,0:T(4,128)} custom-call(f32[24,768]{1,0:T(8,128)} %copy-done, f32[24,768]{1,0:T(8,128)} %copy-done.7, f32[24,768]{1,0:T(8,128)} %copy-done.6, f32[24,768]{1,0:T(8,128)} %copy-done.5, s32[8,768]{1,0:T(8,128)} %constant.4.clone.coord, s32[8,256]{1,0:T(8,128)} %constant.13.clone.home, s32[256,1]{1,0:T(8,128)} %reshape.29.active), custom_call_target="tpu_custom_call" | custom-call | tf_op jit(solution)/shard_map/pallas_call | solution.py:571
  (72 shorter events, 10.5 us)
Async XLA Ops:
  7.1 5.6 %collective-permute-start.2 = (f32[112,64]{1,0:T(8,128)}, f32[112,64]{1,0:T(8,128)S(1)}, u32[]{:S(2)}, u32[]{:S(2)}) collective-permute-start(f32[112,64]{1,0:T(8,128)} %get-tuple-element.17), channel_id=1, source_target_pairs={{0,3},{1,2},{2,1},{3,0},{4,7},{5,6},{6,5},{7,4},{8,11},{9,10},{10,... | collective-permute-start | bytes 86024 | tf_op jit(solution)/shard_map/ppermute | solution.py:612
  9.9 5.9 %collective-permute-start = (f32[112,128]{1,0:T(8,128)}, f32[112,128]{1,0:T(8,128)S(1)}, u32[]{:S(2)}, u32[]{:S(2)}) collective-permute-start(f32[112,128]{1,0:T(8,128)} %get-tuple-element.15), channel_id=1, source_target_pairs={{0,2},{1,3},{2,0},{3,1},{4,6},{5,7},{6,4},{7,5},{8,10},{9,11},{10,... | collective-permute-start | bytes 172040 | tf_op jit(solution)/shard_map/ppermute | solution.py:612
  10.7 4.4 %collective-permute-start.1 = (f32[112,128]{1,0:T(8,128)}, f32[112,128]{1,0:T(8,128)S(1)}, u32[]{:S(2)}, u32[]{:S(2)}) collective-permute-start(f32[112,128]{1,0:T(8,128)} %get-tuple-element.16), channel_id=1, source_target_pairs={{0,1},{1,0},{2,3},{3,2},{4,5},{5,4},{6,7},{7,6},{8,9},{9,8},{10,11... | collective-permute-start | bytes 172040 | tf_op jit(solution)/shard_map/ppermute | solution.py:612
  16.0 4.8 %copy-start.8 = (f32[112,16]{1,0:T(8,128)S(1)}, f32[112,16]{1,0:T(8,128)}, u32[]{:S(2)}) copy-start(f32[112,16]{1,0:T(8,128)} %get-tuple-element.18) | copy-start | bytes 21508
  16.1 6.5 %collective-permute-start.4 = (f32[112,36]{1,0:T(8,128)S(1)}, f32[112,36]{1,0:T(8,128)S(1)}, u32[]{:S(2)}, u32[]{:S(2)}) collective-permute-start(f32[112,36]{1,0:T(8,128)S(1)} %pad_maximum_fusion.1), channel_id=1, source_target_pairs={{0,124},{4,0},{8,4},{12,8},{16,12},{20,16},{24,20},{28,24},{32,28}... | collective-permute-start | bytes 48392 | tf_op jit(solution)/shard_map/ppermute | solution.py:618
  20.8 7.1 %copy-start.3 = (f32[112,256]{1,0:T(8,128)S(1)}, f32[112,256]{1,0:T(8,128)}, u32[]{:S(2)}) copy-start(f32[112,256]{1,0:T(8,128)} %get-tuple-element.14) | copy-start | bytes 344068
  20.9 7.0 %collective-permute-start.3 = (f32[112,36]{1,0:T(8,128)S(1)}, f32[112,36]{1,0:T(8,128)S(1)}, u32[]{:S(2)}, u32[]{:S(2)}) collective-permute-start(f32[112,36]{1,0:T(8,128)S(1)} %pad_maximum_fusion), channel_id=1, source_target_pairs={{0,4},{4,8},{8,12},{12,16},{16,20},{20,24},{24,28},{28,32},{32,36}... | collective-permute-start | bytes 48392 | tf_op jit(solution)/shard_map/ppermute | solution.py:617
  69.0 6.7 %copy-start.10 = (f32[8,768]{1,0:T(8,128)S(1)}, f32[8,768]{1,0:T(8,128)}, u32[]{:S(2)}) copy-start(f32[8,768]{1,0:T(8,128)} %get-tuple-element.21) | copy-start | bytes 73732
  69.8 6.4 %collective-permute-start.5 = (f32[8,72]{1,0:T(8,128)S(1)}, f32[8,72]{1,0:T(8,128)S(1)}, u32[]{:S(2)}, u32[]{:S(2)}) collective-permute-start(f32[8,72]{1,0:T(8,128)S(1)} %get-tuple-element.36), channel_id=1, source_target_pairs={{0,4},{4,8},{8,12},{12,16},{16,20},{20,24},{24,28},{28,32},{32,36}... | collective-permute-start | bytes 6920 | tf_op jit(solution)/shard_map/ppermute | solution.py:637
  69.9 6.4 %collective-permute-start.6 = (f32[8,72]{1,0:T(8,128)S(1)}, f32[8,72]{1,0:T(8,128)S(1)}, u32[]{:S(2)}, u32[]{:S(2)}) collective-permute-start(f32[8,72]{1,0:T(8,128)S(1)} %get-tuple-element.37), channel_id=1, source_target_pairs={{0,124},{4,0},{8,4},{12,8},{16,12},{20,16},{24,20},{28,24},{32,28}... | collective-permute-start | bytes 6920 | tf_op jit(solution)/shard_map/ppermute | solution.py:638
  76.3 4.8 %copy-start.11 = (s32[16,4,4]{0,2,1:T(4,128)S(1)}, s32[16,4,4]{0,2,1:T(4,128)}, u32[]{:S(2)}) copy-start(s32[16,4,4]{0,2,1:T(4,128)} %param.20) | copy-start | bytes 3076
  76.4 5.6 %copy-start.4 = (f32[8,768]{1,0:T(8,128)}, f32[8,768]{1,0:T(8,128)S(1)}, u32[]{:S(2)}) copy-start(f32[8,768]{1,0:T(8,128)S(1)} %pad_maximum_fusion.2.fresh) | copy-start | bytes 73732
  76.4 5.6 %collective-permute-start.9 = (f32[8,768]{1,0:T(8,128)S(1)}, f32[8,768]{1,0:T(8,128)S(1)}, u32[]{:S(2)}, u32[]{:S(2)}) collective-permute-start(f32[8,768]{1,0:T(8,128)S(1)} %pad_maximum_fusion.2.fresh), channel_id=1, source_target_pairs={{0,3},{1,2},{2,1},{3,0},{4,7},{5,6},{6,5},{7,4},{8,11},{9,10},{10,... | collective-permute-start | bytes 73736 | tf_op jit(solution)/shard_map/ppermute | solution.py:631
  76.9 5.2 %collective-permute-start.8 = (f32[8,768]{1,0:T(8,128)S(1)}, f32[8,768]{1,0:T(8,128)S(1)}, u32[]{:S(2)}, u32[]{:S(2)}) collective-permute-start(f32[8,768]{1,0:T(8,128)S(1)} %pad_maximum_fusion.2.fresh), channel_id=1, source_target_pairs={{0,1},{1,0},{2,3},{3,2},{4,5},{5,4},{6,7},{7,6},{8,9},{9,8},{10,11... | collective-permute-start | bytes 73736 | tf_op jit(solution)/shard_map/ppermute | solution.py:631
  77.5 5.7 %collective-permute-start.7 = (f32[8,768]{1,0:T(8,128)S(1)}, f32[8,768]{1,0:T(8,128)S(1)}, u32[]{:S(2)}, u32[]{:S(2)}) collective-permute-start(f32[8,768]{1,0:T(8,128)S(1)} %pad_maximum_fusion.2.fresh), channel_id=1, source_target_pairs={{0,2},{1,3},{2,0},{3,1},{4,6},{5,7},{6,4},{7,5},{8,10},{9,11},{10,... | collective-permute-start | bytes 73736 | tf_op jit(solution)/shard_map/ppermute | solution.py:631
  172.6 4.5 %copy-start.1 = (f32[24,768]{1,0:T(8,128)S(1)}, f32[24,768]{1,0:T(8,128)}, u32[]{:S(2)}) copy-start(f32[24,768]{1,0:T(8,128)} %get-tuple-element.25) | copy-start | bytes 221188
  173.4 2.8 %collective-permute-start.11 = (f32[24,36]{1,0:T(8,128)S(1)}, f32[24,36]{1,0:T(8,128)S(1)}, u32[]{:S(2)}, u32[]{:S(2)}) collective-permute-start(f32[24,36]{1,0:T(8,128)S(1)} %slice.61), channel_id=1, source_target_pairs={{0,124},{4,0},{8,4},{12,8},{16,12},{20,16},{24,20},{28,24},{32,28}... | collective-permute-start | bytes 10376 | tf_op jit(solution)/shard_map/ppermute | solution.py:649
  177.1 6.4 %collective-permute-start.10 = (f32[24,36]{1,0:T(8,128)S(1)}, f32[24,36]{1,0:T(8,128)S(1)}, u32[]{:S(2)}, u32[]{:S(2)}) collective-permute-start(f32[24,36]{1,0:T(8,128)S(1)} %get-tuple-element.27), channel_id=1, source_target_pairs={{0,4},{4,8},{8,12},{12,16},{16,20},{20,24},{24,28},{28,32},{32,36}... | collective-permute-start | bytes 10376 | tf_op jit(solution)/shard_map/ppermute | solution.py:648
  183.7 12.4 %copy-start = (f32[24,768]{1,0:T(8,128)}, f32[24,768]{1,0:T(8,128)S(1)}, u32[]{:S(2)}) copy-start(f32[24,768]{1,0:T(8,128)S(1)} %concatenate.23.pushed) | copy-start | bytes 221188
  183.8 6.7 %collective-permute-start.14 = (f32[24,768]{1,0:T(8,128)S(1)}, f32[24,768]{1,0:T(8,128)S(1)}, u32[]{:S(2)}, u32[]{:S(2)}) collective-permute-start(f32[24,768]{1,0:T(8,128)S(1)} %concatenate.23.pushed), channel_id=1, source_target_pairs={{0,3},{1,2},{2,1},{3,0},{4,7},{5,6},{6,5},{7,4},{8,11},{9,10},{10,... | collective-permute-start | bytes 221192 | tf_op jit(solution)/shard_map/ppermute | solution.py:631
  187.6 5.0 %collective-permute-start.13 = (f32[24,768]{1,0:T(8,128)S(1)}, f32[24,768]{1,0:T(8,128)S(1)}, u32[]{:S(2)}, u32[]{:S(2)}) collective-permute-start(f32[24,768]{1,0:T(8,128)S(1)} %concatenate.23.pushed), channel_id=1, source_target_pairs={{0,1},{1,0},{2,3},{3,2},{4,5},{5,4},{6,7},{7,6},{8,9},{9,8},{10,11... | collective-permute-start | bytes 221192 | tf_op jit(solution)/shard_map/ppermute | solution.py:631
  190.3 5.9 %collective-permute-start.12 = (f32[24,768]{1,0:T(8,128)S(1)}, f32[24,768]{1,0:T(8,128)S(1)}, u32[]{:S(2)}, u32[]{:S(2)}) collective-permute-start(f32[24,768]{1,0:T(8,128)S(1)} %concatenate.23.pushed), channel_id=1, source_target_pairs={{0,2},{1,3},{2,0},{3,1},{4,6},{5,7},{6,4},{7,5},{8,10},{9,11},{10,... | collective-permute-start | bytes 221192 | tf_op jit(solution)/shard_map/ppermute | solution.py:631
  190.5 5.6 %copy-start.5 = (f32[24,768]{1,0:T(8,128)}, f32[24,768]{1,0:T(8,128)S(1)}, u32[]{:S(2)}) copy-start(f32[24,768]{1,0:T(8,128)S(1)} %collective-permute-done.14.pushed_yz) | copy-start | bytes 221188
  192.6 3.5 %copy-start.6 = (f32[24,768]{1,0:T(8,128)}, f32[24,768]{1,0:T(8,128)S(1)}, u32[]{:S(2)}) copy-start(f32[24,768]{1,0:T(8,128)S(1)} %collective-permute-done.13.pushed_z) | copy-start | bytes 221188
  (7 other events, 6.5 us)

commit v4 on v3

--- a/solution.py
+++ b/solution.py
@@ -14,6 +14,8 @@
 CELLS = BX * BY * BZ
 EX, EY, EZ = BX + 2, BY + 2, BZ + 2
 EXT = EX * EY * EZ
+PLANE = EY * EZ
+TOP = BX * PLANE
 LANES = 768
 TILES = LANES // 128
 GROUPS = 2 * LANES
@@ -350,7 +352,7 @@
 
 
 def density_kernel(
-    parts, coord, source, pos, mass, count, table, list_f, count_f, sums,
+    parts, coord, source, pos, mass, count, table, list_f, count_f, sums, low, high,
     list_v, count_v, list_s, items_v, items_s, ends, ends_v, ends_s, rows, columns, total, reduced,
     natural, sem,
 ):
@@ -407,6 +409,8 @@
     run_items(number, BATCH_D, items_s, list_s, item, add)
     scale = 1.0 / (4.0 * math.pi * safe * safe * safe)
     sums[...] = row_sums(total, 0, 1, reduced) * scale
+    low[...] = sums[:, : 2 * PLANE]
+    high[...] = sums[:, TOP:EXT]
 
 
 def joined(sums, along_y, along_z, along_both, coord, shared):
@@ -442,7 +446,7 @@
 
 def force_kernel(
     table, fresh, fresh_y, fresh_z, fresh_yz, list_v, count_v, coord, home, pos, vel, mass, smooth, entropy, stored, count,
-    active, sums, density, list_s, items_v, items_s, ends, ends_v, ends_s, rows, columns, total, reduced,
+    active, sums, density, low, high, list_s, items_v, items_s, ends, ends_v, ends_s, rows, columns, total, reduced,
     natural, sem,
 ):
     list_copy = pltpu.make_async_copy(list_v, list_s, sem.at[0])
@@ -545,6 +549,8 @@
     run_items(number, BATCH_F, items_s, list_s, item, add)
     for c in range(3):
         sums[8 * c : 8 * c + 8, :] = row_sums(total, c, 3, reduced)
+    low[...] = sums[:, :PLANE]
+    high[...] = sums[:, TOP + PLANE : EXT]
 
 
 def spread_kernel(pushed, pushed_y, pushed_z, pushed_yz, coord, home, active, out):
@@ -631,29 +637,22 @@
     return [lax.ppermute(sums, ("gy", "gz"), pairs) for pairs in ACROSS]
 
 
-def shared_sums(sums):
-    plane = EY * EZ
-    top = BX * plane
-    before = lax.ppermute(sums[:, top : top + 2 * plane], "gx", ring("gx", 1))
-    after = lax.ppermute(sums[:, : 2 * plane], "gx", ring("gx", -1))
-    middle = sums[:, 2 * plane : top]
-    return jnp.concatenate(
-        [sums[:, : 2 * plane] + before, middle, sums[:, top:EXT] + after, sums[:, EXT:]], 1
-    )
-
-
-def returned_sums(sums):
-    plane = EY * EZ
-    top = BX * plane
-    before = lax.ppermute(sums[:, top + plane : EXT], "gx", ring("gx", 1))
-    after = lax.ppermute(sums[:, :plane], "gx", ring("gx", -1))
+def shared_sums(sums, low, high):
+    before = lax.ppermute(high, "gx", ring("gx", 1))
+    after = lax.ppermute(low, "gx", ring("gx", -1))
+    return jnp.concatenate([low + before, sums[:, 2 * PLANE : TOP], high + after, sums[:, EXT:]], 1)
+
+
+def returned_sums(sums, low, high):
+    before = lax.ppermute(high, "gx", ring("gx", 1))
+    after = lax.ppermute(low, "gx", ring("gx", -1))
     return jnp.concatenate(
         [
-            sums[:, :plane],
-            sums[:, plane : 2 * plane] + before,
-            sums[:, 2 * plane : top],
-            sums[:, top : top + plane] + after,
-            sums[:, top + plane :],
+            low,
+            sums[:, PLANE : 2 * PLANE] + before,
+            sums[:, 2 * PLANE : TOP],
+            sums[:, TOP : TOP + PLANE] + after,
+            sums[:, TOP + PLANE :],
         ],
         1,
     )
@@ -677,28 +676,28 @@
     widths = (CELLS, 128, 128, 64, 16, 16)
     parts = first_exchange(*call(pack_kernel, inputs, [shape(ROWS, width) for width in widths]))
     inputs = (parts, coord, source, pos, mass, count)
-    table, list_f, count_f, sums = call(
+    table, list_f, count_f, sums, low, high = call(
         density_kernel,
         inputs,
         [
             shape(ROWS, LANES), shape(LIST_ROWS, 128, dtype=i32), shape(16, 128, dtype=i32),
-            shape(ACT, LANES),
+            shape(ACT, LANES), shape(ACT, 2 * PLANE), shape(ACT, 2 * PLANE),
         ],
         scratch=density_scratch(),
     )
-    fresh = shared_sums(sums)
+    fresh = shared_sums(sums, low, high)
     inputs = (
         table, fresh, *sent_across(fresh), list_f, count_f, coord, home, pos, vel, mass, smooth, entropy, stored,
         count, active,
     )
-    sums, density = call(
+    sums, density, low, high = call(
         force_kernel,
         inputs,
-        [shape(24, LANES), shape(BX, BY, BZ, 256)],
+        [shape(24, LANES), shape(BX, BY, BZ, 256), shape(24, PLANE), shape(24, PLANE)],
 
         scratch=force_scratch(),
     )
-    pushed = returned_sums(sums)
+    pushed = returned_sums(sums, low, high)
     inputs = (pushed, *sent_across(pushed), coord, home, active)
     acceleration = call(spread_kernel, inputs, shape(3, BX, BY, BZ, 256))
     return density, acceleration

time: 201 us -> 193 us (0.960)
  Pallas kernels: 136 us -> 132 us
  waiting for transfers between devices: 26.4 us -> 23.5 us
    pallas_call x4, Pallas kernels: 136 us -> 132 us  [call(): pl.pallas_call(kernel, out_shape=outputs, in_specs=in_specs or [VMEM_SPEC...]
    ppermute x4, waiting for transfers between devices: 8.17 us -> 4.98 us  [the longest x1 4.98 us: shared_sums(): before = lax.ppermute(high, 'gx', ring('gx', 1))]
  transfers between devices with their start and end apart: 15 -> 15, of which waited for: 11 -> 10; matrix products, arithmetic and copies ran while one was open for 1% -> 2% of each run, Pallas kernels for 0% -> 0%
where the time goes in v4:
time: 193 us
  Pallas kernels  132 us (68%)
  starting transfers between devices  25.4 us (13%)
  waiting for transfers between devices  23.5 us (12%)
  local copies, waits for them, and re-layouts  7.95 us (4%)
  other arithmetic  2.54 us (1%)
    pallas_call x4, Pallas kernels, call(): pl.pallas_call(kernel, out_shape=outputs, in_specs=in_specs or [VMEM_SPEC...  132 us
    ppermute x6, starting transfers between devices, sent_across(): return [lax.ppermute(sums, ('gy', 'gz'), pairs) for pairs in ACROSS]  10.2 us
    ppermute x6, waiting for transfers between devices, sent_across(): return [lax.ppermute(sums, ('gy', 'gz'), pairs) for pairs in ACROSS]  7.17 us
    ppermute x1, waiting for transfers between devices, first_exchange(): before = lax.ppermute(high, 'gx', ring('gx', 1))  5.29 us
    ppermute x1, starting transfers between devices, returned_sums(): after = lax.ppermute(low, 'gx', ring('gx', -1))  5.05 us
    ppermute x1, waiting for transfers between devices, shared_sums(): before = lax.ppermute(high, 'gx', ring('gx', 1))  4.98 us
    ppermute x1, starting transfers between devices, first_exchange(): after = lax.ppermute(low, 'gx', ring('gx', -1))  4.7 us
    ppermute x3, waiting for transfers between devices, first_exchange(): lax.ppermute(part, ('gy', 'gz'), pairs)  4.47 us
  transfers between devices with their start and end apart: 15, of which 10 were waited for; matrix products, arithmetic and copies ran while one was open for 2% of the time, Pallas kernels for 0%

profile of v4, /device:TPU:0, one launch (start us, length us, event | category | flops | bytes accessed | tf_op | source)
XLA Modules:
  0.0 192.6 jit_solution(13739428363964781195)
XLA Ops:
  3.3 3.7 %shard_map.140 = (f32[112,256]{1,0:T(8,128)}, f32[112,128]{1,0:T(8,128)}, f32[112,128]{1,0:T(8,128)}, f32[112,64]{1,0:T(8,128)}, f32[112,16]{1,0:T(8,128)}, /*index=5*/f32[112,16]{1,0:T(8,128)}) custom-call(f32[3,16,4,4,256]{4,3,2,1,0:T(4,128)} %pos.5, f32[3,16,4,4,256]{4,3,2,1,0:T(4,128)} %vel.3, f32[16,4,4,256]{3,2,1,0:T(4,128)} %mass.5, ...), custom_call_target="tpu_custom_call" | custom-call | tf_op jit(solution)/shard_map/pallas_call | solution.py:577
  7.1 2.8 %collective-permute-start.2 = (f32[112,64]{1,0:T(8,128)}, f32[112,64]{1,0:T(8,128)S(1)}, u32[]{:S(2)}, u32[]{:S(2)}) collective-permute-start(f32[112,64]{1,0:T(8,128)} %get-tuple-element.21), channel_id=1, source_target_pairs={{0,3},{1,2},{2,1},{3,0},{4,7},{5,6},{6,5},{7,4},{8,11},{9,10},{10,... | collective-permute-start | bytes 86024 | tf_op jit(solution)/shard_map/ppermute | solution.py:618
  9.9 0.8 collective-permute-start
  11.2 1.5 collective-permute-done.2
  12.8 2.4 %collective-permute-done.1 = f32[112,128]{1,0:T(8,128)S(1)} collective-permute-done((f32[112,128]{1,0:T(8,128)}, f32[112,128]{1,0:T(8,128)S(1)}, u32[]{:S(2)}, u32[]{:S(2)}) %collective-permute-start.1) | collective-permute-done | bytes 57376 | tf_op jit(solution)/shard_map/ppermute | solution.py:618
  16.1 4.7 %collective-permute-start.4 = (f32[112,36]{1,0:T(8,128)S(1)}, f32[112,36]{1,0:T(8,128)S(1)}, u32[]{:S(2)}, u32[]{:S(2)}) collective-permute-start(f32[112,36]{1,0:T(8,128)S(1)} %pad_maximum_fusion.1), channel_id=1, source_target_pairs={{0,124},{4,0},{8,4},{12,8},{16,12},{20,16},{24,20},{28,24},{32,28}... | collective-permute-start | bytes 48392 | tf_op jit(solution)/shard_map/ppermute | solution.py:624
  21.0 1.6 collective-permute-done.4
  22.7 5.3 %collective-permute-done.3 = f32[112,36]{1,0:T(8,128)S(1)} collective-permute-done((f32[112,36]{1,0:T(8,128)S(1)}, f32[112,36]{1,0:T(8,128)S(1)}, u32[]{:S(2)}, u32[]{:S(2)}) %collective-permute-start.3) | collective-permute-done | bytes 16160 | tf_op jit(solution)/shard_map/ppermute | solution.py:623
  28.0 0.8 concatenate.21.parts
  28.8 37.0 %shard_map.141 = (f32[112,768]{1,0:T(8,128)}, s32[112,128]{1,0:T(8,128)}, s32[16,128]{1,0:T(8,128)}, f32[8,768]{1,0:T(8,128)}, f32[8,72]{1,0:T(8,128)}, /*index=5*/f32[8,72]{1,0:T(8,128)}) custom-call(f32[112,768]{1,0:T(8,128)} %concatenate.21.parts, s32[8,768]{1,0:T(8,128)} %constant.4.clone.coord, s32[8,768]{1,0:T(8,128)} %constant.12.clone.source, ...), custom_call_target="tpu_custom_call" | custom-call | tf_op jit(solution)/shard_map/pallas_call | solution.py:577
  65.8 1.2 collective-permute-start.6
  68.6 5.0 %collective-permute-done.5 = f32[8,72]{1,0:T(8,128)S(1)} collective-permute-done((f32[8,72]{1,0:T(8,128)}, f32[8,72]{1,0:T(8,128)S(1)}, u32[]{:S(2)}, u32[]{:S(2)}) %collective-permute-start.5) | collective-permute-done | bytes 2336 | tf_op jit(solution)/shard_map/ppermute | solution.py:641
  73.7 2.6 %collective-permute-start.9 = (f32[8,768]{1,0:T(8,128)S(1)}, f32[8,768]{1,0:T(8,128)S(1)}, u32[]{:S(2)}, u32[]{:S(2)}) collective-permute-start(f32[8,768]{1,0:T(8,128)S(1)} %pad_maximum_fusion.2.fresh), channel_id=1, source_target_pairs={{0,3},{1,2},{2,1},{3,0},{4,7},{5,6},{6,5},{7,4},{8,11},{9,10},{10,... | collective-permute-start | bytes 73736 | tf_op jit(solution)/shard_map/ppermute | solution.py:637
  76.3 2.4 %collective-permute-start.8 = (f32[8,768]{1,0:T(8,128)S(1)}, f32[8,768]{1,0:T(8,128)S(1)}, u32[]{:S(2)}, u32[]{:S(2)}) collective-permute-start(f32[8,768]{1,0:T(8,128)S(1)} %pad_maximum_fusion.2.fresh), channel_id=1, source_target_pairs={{0,1},{1,0},{2,3},{3,2},{4,5},{5,4},{6,7},{7,6},{8,9},{9,8},{10,11... | collective-permute-start | bytes 73736 | tf_op jit(solution)/shard_map/ppermute | solution.py:637
  80.5 3.5 %collective-permute-done.7.fresh_y = f32[8,768]{1,0:T(8,128)S(1)} collective-permute-done((f32[8,768]{1,0:T(8,128)S(1)}, f32[8,768]{1,0:T(8,128)S(1)}, u32[]{:S(2)}, u32[]{:S(2)}) %collective-permute-start.7) | collective-permute-done | bytes 24608 | tf_op jit(solution)/shard_map/ppermute | solution.py:637
  84.6 88.7 %shard_map.142 = (f32[24,768]{1,0:T(8,128)}, f32[16,4,4,256]{3,2,1,0:T(4,128)}, f32[24,36]{1,0:T(8,128)}, f32[24,36]{1,0:T(8,128)}) custom-call(f32[112,768]{1,0:T(8,128)} %get-tuple-element.24.table, f32[8,768]{1,0:T(8,128)} %copy-done.3, f32[8,768]{1,0:T(8,128)} %copy-done.12, f32[8,768]{1,0:T(8,128)} %copy-done.11, f32[8,768]{1,0:T(8,128)} %copy-done.10, ...), custom_call_target="tpu_custom_call" | custom-call | tf_op jit(solution)/shard_map/pallas_call | solution.py:577
  173.4 5.1 %collective-permute-start.11 = (f32[24,36]{1,0:T(8,128)}, f32[24,36]{1,0:T(8,128)S(1)}, u32[]{:S(2)}, u32[]{:S(2)}) collective-permute-start(f32[24,36]{1,0:T(8,128)} %get-tuple-element.31), channel_id=1, source_target_pairs={{0,124},{4,0},{8,4},{12,8},{16,12},{20,16},{24,20},{28,24},{32,28}... | collective-permute-start | bytes 10376 | tf_op jit(solution)/shard_map/ppermute | solution.py:648
  178.4 0.8 slice.47
  179.2 0.9 slice.45
  181.2 1.9 collective-permute-start.13
  183.1 2.8 %collective-permute-start.12 = (f32[24,768]{1,0:T(8,128)S(1)}, f32[24,768]{1,0:T(8,128)S(1)}, u32[]{:S(2)}, u32[]{:S(2)}) collective-permute-start(f32[24,768]{1,0:T(8,128)S(1)} %concatenate.23.pushed), channel_id=1, source_target_pairs={{0,2},{1,3},{2,0},{3,1},{4,6},{5,7},{6,4},{7,5},{8,10},{9,11},{10,... | collective-permute-start | bytes 221192 | tf_op jit(solution)/shard_map/ppermute | solution.py:637
  185.9 0.9 collective-permute-done.14.pushed_yz
  186.7 2.2 %collective-permute-done.12.pushed_y = f32[24,768]{1,0:T(8,128)S(1)} collective-permute-done((f32[24,768]{1,0:T(8,128)S(1)}, f32[24,768]{1,0:T(8,128)S(1)}, u32[]{:S(2)}, u32[]{:S(2)}) %collective-permute-start.12) | collective-permute-done | bytes 73760 | tf_op jit(solution)/shard_map/ppermute | solution.py:637
  189.6 3.0 %shard_map.143 = f32[3,16,4,4,256]{4,3,2,1,0:T(4,128)} custom-call(f32[24,768]{1,0:T(8,128)} %copy-done, f32[24,768]{1,0:T(8,128)} %copy-done.6, f32[24,768]{1,0:T(8,128)} %copy-done.5, f32[24,768]{1,0:T(8,128)} %copy-done.4, s32[8,768]{1,0:T(8,128)} %constant.4.clone.coord, s32[8,256]{1,0:T(8,128)} %constant.13.clone.home, s32[256,1]{1,0:T(8,128)} %reshape.29.active), custom_call_target="tpu_custom_call" | custom-call | tf_op jit(solution)/shard_map/pallas_call | solution.py:577
  (72 shorter events, 10.2 us)
Async XLA Ops:
  7.1 5.6 %collective-permute-start.2 = (f32[112,64]{1,0:T(8,128)}, f32[112,64]{1,0:T(8,128)S(1)}, u32[]{:S(2)}, u32[]{:S(2)}) collective-permute-start(f32[112,64]{1,0:T(8,128)} %get-tuple-element.21), channel_id=1, source_target_pairs={{0,3},{1,2},{2,1},{3,0},{4,7},{5,6},{6,5},{7,4},{8,11},{9,10},{10,... | collective-permute-start | bytes 86024 | tf_op jit(solution)/shard_map/ppermute | solution.py:618
  9.9 5.9 %collective-permute-start = (f32[112,128]{1,0:T(8,128)}, f32[112,128]{1,0:T(8,128)S(1)}, u32[]{:S(2)}, u32[]{:S(2)}) collective-permute-start(f32[112,128]{1,0:T(8,128)} %get-tuple-element.19), channel_id=1, source_target_pairs={{0,2},{1,3},{2,0},{3,1},{4,6},{5,7},{6,4},{7,5},{8,10},{9,11},{10,... | collective-permute-start | bytes 172040 | tf_op jit(solution)/shard_map/ppermute | solution.py:618
  10.7 4.4 %collective-permute-start.1 = (f32[112,128]{1,0:T(8,128)}, f32[112,128]{1,0:T(8,128)S(1)}, u32[]{:S(2)}, u32[]{:S(2)}) collective-permute-start(f32[112,128]{1,0:T(8,128)} %get-tuple-element.20), channel_id=1, source_target_pairs={{0,1},{1,0},{2,3},{3,2},{4,5},{5,4},{6,7},{7,6},{8,9},{9,8},{10,11... | collective-permute-start | bytes 172040 | tf_op jit(solution)/shard_map/ppermute | solution.py:618
  16.0 4.8 %copy-start.7 = (f32[112,16]{1,0:T(8,128)S(1)}, f32[112,16]{1,0:T(8,128)}, u32[]{:S(2)}) copy-start(f32[112,16]{1,0:T(8,128)} %get-tuple-element.22) | copy-start | bytes 21508
  16.1 6.5 %collective-permute-start.4 = (f32[112,36]{1,0:T(8,128)S(1)}, f32[112,36]{1,0:T(8,128)S(1)}, u32[]{:S(2)}, u32[]{:S(2)}) collective-permute-start(f32[112,36]{1,0:T(8,128)S(1)} %pad_maximum_fusion.1), channel_id=1, source_target_pairs={{0,124},{4,0},{8,4},{12,8},{16,12},{20,16},{24,20},{28,24},{32,28}... | collective-permute-start | bytes 48392 | tf_op jit(solution)/shard_map/ppermute | solution.py:624
  20.8 7.1 %copy-start.2 = (f32[112,256]{1,0:T(8,128)S(1)}, f32[112,256]{1,0:T(8,128)}, u32[]{:S(2)}) copy-start(f32[112,256]{1,0:T(8,128)} %get-tuple-element.18) | copy-start | bytes 344068
  20.9 7.0 %collective-permute-start.3 = (f32[112,36]{1,0:T(8,128)S(1)}, f32[112,36]{1,0:T(8,128)S(1)}, u32[]{:S(2)}, u32[]{:S(2)}) collective-permute-start(f32[112,36]{1,0:T(8,128)S(1)} %pad_maximum_fusion), channel_id=1, source_target_pairs={{0,4},{4,8},{8,12},{12,16},{16,20},{20,24},{24,28},{28,32},{32,36}... | collective-permute-start | bytes 48392 | tf_op jit(solution)/shard_map/ppermute | solution.py:623
  65.8 2.7 %collective-permute-start.6 = (f32[8,72]{1,0:T(8,128)}, f32[8,72]{1,0:T(8,128)S(1)}, u32[]{:S(2)}, u32[]{:S(2)}) collective-permute-start(f32[8,72]{1,0:T(8,128)} %get-tuple-element.25), channel_id=1, source_target_pairs={{0,124},{4,0},{8,4},{12,8},{16,12},{20,16},{24,20},{28,24},{32,28}... | collective-permute-start | bytes 6920 | tf_op jit(solution)/shard_map/ppermute | solution.py:642
  67.0 6.6 %collective-permute-start.5 = (f32[8,72]{1,0:T(8,128)}, f32[8,72]{1,0:T(8,128)S(1)}, u32[]{:S(2)}, u32[]{:S(2)}) collective-permute-start(f32[8,72]{1,0:T(8,128)} %get-tuple-element.26), channel_id=1, source_target_pairs={{0,4},{4,8},{8,12},{12,16},{16,20},{20,24},{24,28},{28,32},{32,36}... | collective-permute-start | bytes 6920 | tf_op jit(solution)/shard_map/ppermute | solution.py:641
  68.6 5.0 %copy-start.15 = (f32[8,72]{1,0:T(8,128)S(1)}, f32[8,72]{1,0:T(8,128)}, u32[]{:S(2)}) copy-start(f32[8,72]{1,0:T(8,128)} %get-tuple-element.25) | copy-start | bytes 6916
  73.6 5.5 %copy-start.9 = (s32[16,4,4]{0,2,1:T(4,128)S(1)}, s32[16,4,4]{0,2,1:T(4,128)}, u32[]{:S(2)}) copy-start(s32[16,4,4]{0,2,1:T(4,128)} %param.20) | copy-start | bytes 3076
  73.6 6.3 %copy-start.3 = (f32[8,768]{1,0:T(8,128)}, f32[8,768]{1,0:T(8,128)S(1)}, u32[]{:S(2)}) copy-start(f32[8,768]{1,0:T(8,128)S(1)} %pad_maximum_fusion.2.fresh) | copy-start | bytes 73732
  73.7 6.3 %collective-permute-start.9 = (f32[8,768]{1,0:T(8,128)S(1)}, f32[8,768]{1,0:T(8,128)S(1)}, u32[]{:S(2)}, u32[]{:S(2)}) collective-permute-start(f32[8,768]{1,0:T(8,128)S(1)} %pad_maximum_fusion.2.fresh), channel_id=1, source_target_pairs={{0,3},{1,2},{2,1},{3,0},{4,7},{5,6},{6,5},{7,4},{8,11},{9,10},{10,... | collective-permute-start | bytes 73736 | tf_op jit(solution)/shard_map/ppermute | solution.py:637
  76.3 4.2 %collective-permute-start.8 = (f32[8,768]{1,0:T(8,128)S(1)}, f32[8,768]{1,0:T(8,128)S(1)}, u32[]{:S(2)}, u32[]{:S(2)}) collective-permute-start(f32[8,768]{1,0:T(8,128)S(1)} %pad_maximum_fusion.2.fresh), channel_id=1, source_target_pairs={{0,1},{1,0},{2,3},{3,2},{4,5},{5,4},{6,7},{7,6},{8,9},{9,8},{10,11... | collective-permute-start | bytes 73736 | tf_op jit(solution)/shard_map/ppermute | solution.py:637
  78.7 5.3 %collective-permute-start.7 = (f32[8,768]{1,0:T(8,128)S(1)}, f32[8,768]{1,0:T(8,128)S(1)}, u32[]{:S(2)}, u32[]{:S(2)}) collective-permute-start(f32[8,768]{1,0:T(8,128)S(1)} %pad_maximum_fusion.2.fresh), channel_id=1, source_target_pairs={{0,2},{1,3},{2,0},{3,1},{4,6},{5,7},{6,4},{7,5},{8,10},{9,11},{10,... | collective-permute-start | bytes 73736 | tf_op jit(solution)/shard_map/ppermute | solution.py:637
  79.9 4.1 %copy-start.10 = (f32[8,768]{1,0:T(8,128)}, f32[8,768]{1,0:T(8,128)S(1)}, u32[]{:S(2)}) copy-start(f32[8,768]{1,0:T(8,128)S(1)} %collective-permute-done.9.fresh_yz) | copy-start | bytes 73732
  80.5 3.5 %copy-start.11 = (f32[8,768]{1,0:T(8,128)}, f32[8,768]{1,0:T(8,128)S(1)}, u32[]{:S(2)}) copy-start(f32[8,768]{1,0:T(8,128)S(1)} %collective-permute-done.8.fresh_z) | copy-start | bytes 73732
  173.3 6.9 %collective-permute-start.10 = (f32[24,36]{1,0:T(8,128)}, f32[24,36]{1,0:T(8,128)S(1)}, u32[]{:S(2)}, u32[]{:S(2)}) collective-permute-start(f32[24,36]{1,0:T(8,128)} %get-tuple-element.33), channel_id=1, source_target_pairs={{0,4},{4,8},{8,12},{12,16},{16,20},{20,24},{24,28},{28,32},{32,36}... | collective-permute-start | bytes 10376 | tf_op jit(solution)/shard_map/ppermute | solution.py:647
  173.4 6.8 %collective-permute-start.11 = (f32[24,36]{1,0:T(8,128)}, f32[24,36]{1,0:T(8,128)S(1)}, u32[]{:S(2)}, u32[]{:S(2)}) collective-permute-start(f32[24,36]{1,0:T(8,128)} %get-tuple-element.31), channel_id=1, source_target_pairs={{0,124},{4,0},{8,4},{12,8},{16,12},{20,16},{24,20},{28,24},{32,28}... | collective-permute-start | bytes 10376 | tf_op jit(solution)/shard_map/ppermute | solution.py:648
  181.1 7.9 %copy-start = (f32[24,768]{1,0:T(8,128)}, f32[24,768]{1,0:T(8,128)S(1)}, u32[]{:S(2)}) copy-start(f32[24,768]{1,0:T(8,128)S(1)} %concatenate.23.pushed) | copy-start | bytes 221188
  181.1 5.6 %collective-permute-start.14 = (f32[24,768]{1,0:T(8,128)S(1)}, f32[24,768]{1,0:T(8,128)S(1)}, u32[]{:S(2)}, u32[]{:S(2)}) collective-permute-start(f32[24,768]{1,0:T(8,128)S(1)} %concatenate.23.pushed), channel_id=1, source_target_pairs={{0,3},{1,2},{2,1},{3,0},{4,7},{5,6},{6,5},{7,4},{8,11},{9,10},{10,... | collective-permute-start | bytes 221192 | tf_op jit(solution)/shard_map/ppermute | solution.py:637
  181.2 5.6 %collective-permute-start.13 = (f32[24,768]{1,0:T(8,128)S(1)}, f32[24,768]{1,0:T(8,128)S(1)}, u32[]{:S(2)}, u32[]{:S(2)}) collective-permute-start(f32[24,768]{1,0:T(8,128)S(1)} %concatenate.23.pushed), channel_id=1, source_target_pairs={{0,1},{1,0},{2,3},{3,2},{4,5},{5,4},{6,7},{7,6},{8,9},{9,8},{10,11... | collective-permute-start | bytes 221192 | tf_op jit(solution)/shard_map/ppermute | solution.py:637
  183.1 5.9 %collective-permute-start.12 = (f32[24,768]{1,0:T(8,128)S(1)}, f32[24,768]{1,0:T(8,128)S(1)}, u32[]{:S(2)}, u32[]{:S(2)}) collective-permute-start(f32[24,768]{1,0:T(8,128)S(1)} %concatenate.23.pushed), channel_id=1, source_target_pairs={{0,2},{1,3},{2,0},{3,1},{4,6},{5,7},{6,4},{7,5},{8,10},{9,11},{10,... | collective-permute-start | bytes 221192 | tf_op jit(solution)/shard_map/ppermute | solution.py:637
  186.7 2.3 %copy-start.4 = (f32[24,768]{1,0:T(8,128)}, f32[24,768]{1,0:T(8,128)S(1)}, u32[]{:S(2)}) copy-start(f32[24,768]{1,0:T(8,128)S(1)} %collective-permute-done.14.pushed_yz) | copy-start | bytes 221188
  (8 other events, 8.0 us)
